TPU v7x, 32 devices: a whole 2x2x4 slice. The times are simulated.
32 devices in a mesh: blk: 16 (over z, x, core), ctx: 2 (over y).
Axes of the slice: x: 2, y: 2, z: 4, core: 2. Of those that a mesh axis runs over, the one named last changes fastest.
Arguments:
- inputs: bfloat16 [4096, 2048], P(('blk', 'ctx')), may hold values from -6 to 6
- out_grad: bfloat16 [4096, 2048], P(('blk', 'ctx')), may hold values from -6 to 6
- seq_lengths: int32 [16], replicated, may hold values from 1 to 1024, 4096 in all
- key_live: int32 [4096], replicated, may hold values 0 or 1
- attn_gain: bfloat16 [2048], P(('blk', 'ctx')), may hold values from 0.5 to 1.5
- q_down: bfloat16 [2048, 1024], P(('blk', 'ctx')), may hold values from -0.125 to 0.125
- q_gain: bfloat16 [1024], P(('blk', 'ctx')), may hold values from 0.5 to 1.5
- q_up: bfloat16 [1024, 4096], P(('blk', 'ctx')), may hold values from -0.1875 to 0.1875
- k_proj: bfloat16 [2048, 256], P(('blk', 'ctx')), may hold values from -0.125 to 0.125
- v_proj: bfloat16 [2048, 256], P(('blk', 'ctx')), may hold values from -0.125 to 0.125
- o_proj: bfloat16 [4096, 2048], P(('blk', 'ctx')), may hold values from -1.5 to 1.5
- ffn_gain: bfloat16 [2048], P(('blk', 'ctx')), may hold values from 0.5 to 1.5
- w_gate: bfloat16 [2048, 5632], P(('blk', 'ctx')), may hold values from -0.125 to 0.125
- w_up: bfloat16 [2048, 5632], P(('blk', 'ctx')), may hold values from -0.125 to 0.125
- w_down: bfloat16 [5632, 2048], P(('blk', 'ctx')), may hold values from -0.078125 to 0.078125
Outputs:
- output: bfloat16 [4096, 2048], P(('blk', 'ctx'))
- input_grad: float32 [4096, 2048], P(('blk', 'ctx'))
- attn_gain_grad: float32 [2048], P(('blk', 'ctx'))
- q_down_grad: float32 [2048, 1024], P(('blk', 'ctx'))
- q_gain_grad: float32 [1024], P(('blk', 'ctx'))
- q_up_grad: float32 [1024, 4096], P(('blk', 'ctx'))
- k_proj_grad: float32 [2048, 256], P(('blk', 'ctx'))
- v_proj_grad: float32 [2048, 256], P(('blk', 'ctx'))
- o_proj_grad: float32 [4096, 2048], P(('blk', 'ctx'))
- ffn_gain_grad: float32 [2048], P(('blk', 'ctx'))
- w_gate_grad: float32 [2048, 5632], P(('blk', 'ctx'))
- w_up_grad: float32 [2048, 5632], P(('blk', 'ctx'))
- w_down_grad: float32 [5632, 2048], P(('blk', 'ctx'))
Inputs may be any that keep to these rules, and one draw needn't show every extreme that they name: `seq_lengths`: 16 sequences packed in order, heavy-tailed lengths summing to 4096; the longest is exactly 1024.
All inputs are finite; a program needn't handle non-finite values.
Results may differ from a plain program's by a relative error of at most 0.015.
Values may be sent and summed in bfloat16 or wider, within the bound.
No kernel may reach another device: no remote copies, remote signals or barrier semaphores. Data moves between devices by JAX's collectives and lax.ppermute only.
A program may use at most 448 MiB of HBM per device.

v0:
```python
import jax
import jax.numpy as jnp
from jax import lax
from jax.sharding import PartitionSpec as P

H = 16
HD = 256
REACH = 4


EPSILON = 1e-06
ROPE_BASE = 10000.0
NEGATIVE = -1e30


def passed_along(value, axis, steps):
    count = lax.axis_size(axis)
    leading, last = (max(0, -steps), min(count, count - steps))
    return lax.ppermute(value, axis, [(source, source + steps) for source in range(leading, last)])


def token_tables(seq_lengths, token_index):
    seq_ends = jnp.cumsum(seq_lengths)
    passed = seq_ends[None, :] <= token_index[:, None]
    segment = jnp.sum(passed.astype(jnp.int32), axis=1)
    seq_start = jnp.sum(jnp.where(passed, seq_lengths[None, :], 0), axis=1)
    return (segment, token_index - seq_start)


def rope_tables(position, head_width):
    half_width = head_width // 2
    frequency = ROPE_BASE ** (-(2.0 * jnp.arange(half_width, dtype=jnp.float32)) / head_width)
    angles = position.astype(jnp.float32)[:, None] * frequency[None, :]
    return (jnp.cos(angles), jnp.sin(angles))


def rotate(source, cosines, sines):
    half_width = source.shape[-1] // 2
    first = source[..., :half_width]
    second = source[..., half_width:]
    return jnp.concatenate(
        [first * cosines - second * sines, second * cosines + first * sines], axis=-1
    )


def norm_forward(source, gain_row):
    inv_rms = lax.rsqrt(jnp.mean(source * source, axis=-1, keepdims=True) + EPSILON)
    return (source * inv_rms * gain_row, inv_rms)


def norm_backward(source, inv_rms, gain_row, cotangent):
    weighted = cotangent * gain_row
    d_source = inv_rms * weighted - source * inv_rms**3 * jnp.mean(
        weighted * source, axis=-1, keepdims=True
    )
    d_gain = jnp.sum(cotangent * source * inv_rms, axis=0)
    return (d_source, d_gain)


def product(left, right):
    return jnp.dot(left, right, preferred_element_type=jnp.float32)


def shards(
    inputs,
    out_grad,
    seq_lengths,
    key_live,
    attn_gain,
    q_down,
    q_gain,
    q_up,
    k_proj,
    v_proj,
    o_proj,
    ffn_gain,
    w_gate,
    w_up,
    w_down,
):
    tok_rows = inputs.shape[0]
    ctx_count = lax.axis_size("ctx")
    pair_rows = tok_rows * ctx_count
    blk_index = lax.axis_index("blk")
    scale = HD ** (-0.5)
    offset = (blk_index * ctx_count + lax.axis_index("ctx")) * tok_rows
    q_index = offset + jnp.arange(tok_rows, dtype=jnp.int32)
    q_segment, q_position = token_tables(seq_lengths, q_index)
    cosines, sines = rope_tables(q_position, HD)
    key_span = (REACH + 1) * pair_rows
    k_index = (blk_index - REACH) * pair_rows + jnp.arange(key_span, dtype=jnp.int32)
    k_clip = jnp.maximum(k_index, 0)
    k_segment, unused = token_tables(seq_lengths, k_clip)
    k_live = jnp.take(key_live, k_clip)
    visible = (k_segment[None, :] == q_segment[:, None]) & (k_index[None, :] <= q_index[:, None])
    visible = visible & ((k_live[None, :] == 1) | (k_index[None, :] == q_index[:, None]))
    visible = visible & (k_index[None, :] >= 0)
    attn_parts = (attn_gain, q_gain, q_down, q_up, k_proj, v_proj, o_proj)
    ffn_parts = (ffn_gain, w_gate, w_up, w_down)
    gain_attn, gain_query, full_qd, full_qu, full_k, full_v, full_o = (
        lax.all_gather(attn_parts[0], ("blk", "ctx"), axis=0, tiled=True),
        lax.all_gather(attn_parts[1], ("blk", "ctx"), axis=0, tiled=True),
        lax.all_gather(attn_parts[2], ("blk", "ctx"), axis=0, tiled=True),
        lax.all_gather(attn_parts[3], ("blk", "ctx"), axis=0, tiled=True),
        lax.all_gather(attn_parts[4], ("blk", "ctx"), axis=0, tiled=True),
        lax.all_gather(attn_parts[5], ("blk", "ctx"), axis=0, tiled=True),
        lax.all_gather(attn_parts[6], ("blk", "ctx"), axis=0, tiled=True),
    )
    x_float = inputs.astype(jnp.float32)
    normed_float, x_inv = norm_forward(x_float, gain_attn.astype(jnp.float32))
    normed = normed_float.astype(jnp.bfloat16)
    latent = product(normed, full_qd)
    latent_float, latent_inv = norm_forward(latent, gain_query.astype(jnp.float32))
    latent_low = latent_float.astype(jnp.bfloat16)
    q_pre = product(latent_low, full_qu).reshape(tok_rows, H, HD)
    queries = rotate(q_pre, cosines[:, None, :], sines[:, None, :]).astype(jnp.bfloat16)
    key_rows = rotate(product(normed, full_k), cosines, sines).astype(jnp.bfloat16)
    values = product(normed, full_v).astype(jnp.bfloat16)
    pair_block = lax.all_gather(
        jnp.concatenate([key_rows, values], axis=1), "ctx", axis=0, tiled=True
    )
    received = [pair_block]
    moving = pair_block
    for cycle_step in range(REACH):
        moving = passed_along(moving, "blk", 1)
        received.append(moving)
    window = jnp.concatenate(received[::-1], axis=0)
    win_keys = window[:, :HD]
    win_values = window[:, HD:]
    block_rows = min(tok_rows, max(1, 512 // H))
    block_count = tok_rows // block_rows
    q_blocks = queries.reshape(block_count, block_rows, H, HD)
    vis_blocks = visible.reshape(block_count, block_rows, key_span)

    def attend(block_item):
        q_part, vis_part = block_item
        scores = (
            jnp.einsum("thd,kd->thk", q_part, win_keys, preferred_element_type=jnp.float32) * scale
        )
        scores = jnp.where(vis_part[:, None, :], scores, NEGATIVE)
        row_max = jnp.max(scores, axis=-1, keepdims=True)
        exp_scores = jnp.exp(scores - row_max)
        denominator = jnp.sum(exp_scores, axis=-1, keepdims=True)
        prob_low = (exp_scores / denominator).astype(jnp.bfloat16)
        result = jnp.einsum("thk,kd->thd", prob_low, win_values, preferred_element_type=jnp.float32)
        return (result, (row_max + jnp.log(denominator))[..., 0])

    attended, log_total = lax.map(attend, (q_blocks, vis_blocks))
    attended = attended.reshape(tok_rows, H * HD).astype(jnp.bfloat16)
    middle = x_float + product(attended, full_o)
    gain_ffn, full_gate, full_up, full_down = (
        lax.all_gather(ffn_parts[0], ("blk", "ctx"), axis=0, tiled=True),
        lax.all_gather(ffn_parts[1], ("blk", "ctx"), axis=0, tiled=True),
        lax.all_gather(ffn_parts[2], ("blk", "ctx"), axis=0, tiled=True),
        lax.all_gather(ffn_parts[3], ("blk", "ctx"), axis=0, tiled=True),
    )
    mid_float, mid_inv = norm_forward(middle, gain_ffn.astype(jnp.float32))
    normed_mid = mid_float.astype(jnp.bfloat16)
    gate_act = product(normed_mid, full_gate)
    up_act = product(normed_mid, full_up)
    sigmoid_gate = jax.nn.sigmoid(gate_act)
    silu_gate = gate_act * sigmoid_gate
    hidden = (silu_gate * up_act).astype(jnp.bfloat16)
    output = (middle + product(hidden, full_down)).astype(jnp.bfloat16)
    gain_ffn, full_gate, full_up, full_down = (
        lax.all_gather(ffn_parts[0], ("blk", "ctx"), axis=0, tiled=True),
        lax.all_gather(ffn_parts[1], ("blk", "ctx"), axis=0, tiled=True),
        lax.all_gather(ffn_parts[2], ("blk", "ctx"), axis=0, tiled=True),
        lax.all_gather(ffn_parts[3], ("blk", "ctx"), axis=0, tiled=True),
    )
    d_hidden = jnp.einsum("td,fd->tf", out_grad, full_down, preferred_element_type=jnp.float32)
    grad_down = jnp.einsum("tf,td->fd", hidden, out_grad, preferred_element_type=jnp.float32)
    d_gate = (d_hidden * up_act * sigmoid_gate * (1.0 + gate_act * (1.0 - sigmoid_gate))).astype(
        jnp.bfloat16
    )
    d_up = (d_hidden * silu_gate).astype(jnp.bfloat16)
    grad_gate = jnp.einsum("td,tf->df", normed_mid, d_gate, preferred_element_type=jnp.float32)
    grad_up = jnp.einsum("td,tf->df", normed_mid, d_up, preferred_element_type=jnp.float32)
    d_normed_mid = jnp.einsum("tf,df->td", d_gate, full_gate, preferred_element_type=jnp.float32)
    d_normed_mid = d_normed_mid + jnp.einsum(
        "tf,df->td", d_up, full_up, preferred_element_type=jnp.float32
    )
    d_mid_norm, grad_gain_ffn = norm_backward(
        middle, mid_inv, gain_ffn.astype(jnp.float32), d_normed_mid
    )
    d_middle = out_grad.astype(jnp.float32) + d_mid_norm
    ffn_sums = (
        lax.psum_scatter(grad_gain_ffn, ("blk", "ctx"), scatter_dimension=0, tiled=True),
        lax.psum_scatter(grad_gate, ("blk", "ctx"), scatter_dimension=0, tiled=True),
        lax.psum_scatter(grad_up, ("blk", "ctx"), scatter_dimension=0, tiled=True),
        lax.psum_scatter(grad_down, ("blk", "ctx"), scatter_dimension=0, tiled=True),
    )
    gain_attn, gain_query, full_qd, full_qu, full_k, full_v, full_o = (
        lax.all_gather(attn_parts[0], ("blk", "ctx"), axis=0, tiled=True),
        lax.all_gather(attn_parts[1], ("blk", "ctx"), axis=0, tiled=True),
        lax.all_gather(attn_parts[2], ("blk", "ctx"), axis=0, tiled=True),
        lax.all_gather(attn_parts[3], ("blk", "ctx"), axis=0, tiled=True),
        lax.all_gather(attn_parts[4], ("blk", "ctx"), axis=0, tiled=True),
        lax.all_gather(attn_parts[5], ("blk", "ctx"), axis=0, tiled=True),
        lax.all_gather(attn_parts[6], ("blk", "ctx"), axis=0, tiled=True),
    )
    d_middle_low = d_middle.astype(jnp.bfloat16)
    grad_o = jnp.einsum("tc,td->cd", attended, d_middle_low, preferred_element_type=jnp.float32)
    d_attended = jnp.einsum(
        "td,cd->tc", d_middle_low, full_o, preferred_element_type=jnp.float32
    ).astype(jnp.bfloat16)
    d_blocks = d_attended.reshape(block_count, block_rows, H, HD)

    def attend_back(totals, block_item):
        q_part, vis_part, lse_part, d_part = block_item
        scores = (
            jnp.einsum("thd,kd->thk", q_part, win_keys, preferred_element_type=jnp.float32) * scale
        )
        scores = jnp.where(vis_part[:, None, :], scores, NEGATIVE)
        soft = jnp.exp(scores - lse_part[..., None])
        prob_low = (soft / jnp.sum(soft, axis=-1, keepdims=True)).astype(jnp.bfloat16)
        d_probs = jnp.einsum("thd,kd->thk", d_part, win_values, preferred_element_type=jnp.float32)
        d_scores = (soft * (d_probs - jnp.sum(soft * d_probs, axis=-1, keepdims=True))).astype(
            jnp.bfloat16
        )
        d_query = (
            jnp.einsum("thk,kd->thd", d_scores, win_keys, preferred_element_type=jnp.float32)
            * scale
        )
        d_keys = (
            totals[0]
            + jnp.einsum("thk,thd->kd", d_scores, q_part, preferred_element_type=jnp.float32)
            * scale
        )
        d_values = totals[1] + jnp.einsum(
            "thk,thd->kd", prob_low, d_part, preferred_element_type=jnp.float32
        )
        return ((d_keys, d_values), d_query)

    zero_rows = jnp.zeros((key_span, HD), jnp.float32)
    (d_win_keys, d_win_values), d_queries = lax.scan(
        attend_back, (zero_rows, zero_rows), (q_blocks, vis_blocks, log_total, d_blocks)
    )
    pieces = jnp.concatenate([d_win_keys, d_win_values], axis=1).reshape(
        REACH + 1, pair_rows, 2 * HD
    )
    carried = pieces[0]
    for cycle_step in range(REACH):
        carried = passed_along(carried, "blk", -1) + pieces[cycle_step + 1]
    own_grads = lax.psum_scatter(carried, "ctx", scatter_dimension=0, tiled=True)
    dk_low = rotate(own_grads[:, :HD], cosines, -sines).astype(jnp.bfloat16)
    dv_low = own_grads[:, HD:].astype(jnp.bfloat16)
    d_queries = d_queries.reshape(tok_rows, H, HD)
    dq_low = (
        rotate(d_queries, cosines[:, None, :], -sines[:, None, :])
        .astype(jnp.bfloat16)
        .reshape(tok_rows, H * HD)
    )
    grad_qu = jnp.einsum("tr,tc->rc", latent_low, dq_low, preferred_element_type=jnp.float32)
    d_latent_low = jnp.einsum("tc,rc->tr", dq_low, full_qu, preferred_element_type=jnp.float32)
    d_latent, grad_gain_query = norm_backward(
        latent, latent_inv, gain_query.astype(jnp.float32), d_latent_low
    )
    dlat_low = d_latent.astype(jnp.bfloat16)
    grad_qd = jnp.einsum("td,tr->dr", normed, dlat_low, preferred_element_type=jnp.float32)
    grad_k = jnp.einsum("td,te->de", normed, dk_low, preferred_element_type=jnp.float32)
    grad_v = jnp.einsum("td,te->de", normed, dv_low, preferred_element_type=jnp.float32)
    d_normed = jnp.einsum("tr,dr->td", dlat_low, full_qd, preferred_element_type=jnp.float32)
    d_normed = d_normed + jnp.einsum(
        "te,de->td", dk_low, full_k, preferred_element_type=jnp.float32
    )
    d_normed = d_normed + jnp.einsum(
        "te,de->td", dv_low, full_v, preferred_element_type=jnp.float32
    )
    d_x_norm, grad_gain_attn = norm_backward(
        x_float, x_inv, gain_attn.astype(jnp.float32), d_normed
    )
    input_grad = d_middle + d_x_norm
    attn_sums = (
        lax.psum_scatter(grad_gain_attn, ("blk", "ctx"), scatter_dimension=0, tiled=True),
        lax.psum_scatter(grad_gain_query, ("blk", "ctx"), scatter_dimension=0, tiled=True),
        lax.psum_scatter(grad_qd, ("blk", "ctx"), scatter_dimension=0, tiled=True),
        lax.psum_scatter(grad_qu, ("blk", "ctx"), scatter_dimension=0, tiled=True),
        lax.psum_scatter(grad_k, ("blk", "ctx"), scatter_dimension=0, tiled=True),
        lax.psum_scatter(grad_v, ("blk", "ctx"), scatter_dimension=0, tiled=True),
        lax.psum_scatter(grad_o, ("blk", "ctx"), scatter_dimension=0, tiled=True),
    )
    return (
        output,
        input_grad,
        attn_sums[0],
        attn_sums[2],
        attn_sums[1],
        attn_sums[3],
        attn_sums[4],
        attn_sums[5],
        attn_sums[6],
        ffn_sums[0],
        ffn_sums[1],
        ffn_sums[2],
        ffn_sums[3],
    )


def solution(mesh):
    placed = (
        P(("blk", "ctx"), None),
        P(("blk", "ctx"), None),
        P(),
        P(),
        P(("blk", "ctx")),
        P(("blk", "ctx"), None),
        P(("blk", "ctx")),
        P(("blk", "ctx"), None),
        P(("blk", "ctx"), None),
        P(("blk", "ctx"), None),
        P(("blk", "ctx"), None),
        P(("blk", "ctx")),
        P(("blk", "ctx"), None),
        P(("blk", "ctx"), None),
        P(("blk", "ctx"), None),
    )
    return jax.shard_map(
        shards,
        mesh=mesh,
        in_specs=placed,
        out_specs=(
            P(("blk", "ctx"), None),
            P(("blk", "ctx"), None),
            P(("blk", "ctx")),
            P(("blk", "ctx"), None),
            P(("blk", "ctx")),
            P(("blk", "ctx"), None),
            P(("blk", "ctx"), None),
            P(("blk", "ctx"), None),
            P(("blk", "ctx"), None),
            P(("blk", "ctx")),
            P(("blk", "ctx"), None),
            P(("blk", "ctx"), None),
            P(("blk", "ctx"), None),
        ),
        check_vma=False,
    )
```

profile of v0, /device:TPU:0, one launch (start us, length us, event | category | flops | bytes accessed | tf_op | source)
XLA Modules:
  0.0 5449.8 jit_solution(2224232565630036737)
XLA Ops:
  13.8 42.2 all-reduce.7
  56.8 10.6 all-gather.13.cloned.1.call-done
  70.0 53.0 all-gather.15.cloned.1.call-done
  124.7 6.4 all_gather.53
  133.5 6.4 collective-permute-start.1
  141.0 6.5 collective-permute-start.2
  147.7 7.1 gather_fusion
  154.8 4.4 collective-permute-start.3
  161.7 28.1 all-gather.9.cloned.1.call-done
  193.4 75.4 %all-gather.11.cloned.1.call-done = bf16[1024,4096]{1,0:T(8,128)(2,1)} async-done(((bf16[32,4096]{1,0:T(8,128)(2,1)}), bf16[1024,4096]{1,0:T(8,128)(2,1)}) %all-gather.11.cloned.1.call-update) | async-done | bytes 8388624 | tf_op jit(solution)/shard_map/all_gather | solution.py:104
  268.8 4.7 fusion.85
  274.7 16.1 while.29
  292.9 92.1 %all-gather.17.cloned.1.call-done = bf16[4096,2048]{1,0:T(8,128)(2,1)} async-done(((bf16[128,2048]{1,0:T(8,128)(2,1)}), bf16[4096,2048]{1,0:T(8,128)(2,1)}) %all-gather.17.cloned.1.call-update) | async-done | bytes 16777232 | tf_op jit(solution)/shard_map/all_gather | solution.py:107
  385.0 8.2 multiply_reduce_fusion.3
  393.4 137.1 %all-gather.19.cloned.1.call-done = bf16[2048,5632]{1,0:T(8,128)(2,1)} async-done(((bf16[64,5632]{1,0:T(8,128)(2,1)}), bf16[2048,5632]{1,0:T(8,128)(2,1)}) %all-gather.19.cloned.1.call-update) | async-done | bytes 23068688 | tf_op jit(solution)/shard_map/all_gather | solution.py:153
  530.6 12.4 fusion.97
  543.0 133.3 %all-gather.21.cloned.1.call-done = bf16[2048,5632]{1,0:T(8,128)(2,1)} async-done(((bf16[64,5632]{1,0:T(8,128)(2,1)}), bf16[2048,5632]{1,0:T(8,128)(2,1)}) %all-gather.21.cloned.1.call-update) | async-done | bytes 23068688 | tf_op jit(solution)/shard_map/all_gather | solution.py:154
  676.3 12.3 fusion.98
  688.6 133.4 %all-gather.23.cloned.1.call-done = bf16[5632,2048]{1,0:T(8,128)(2,1)} async-done(((bf16[176,2048]{1,0:T(8,128)(2,1)}), bf16[5632,2048]{1,0:T(8,128)(2,1)}) %all-gather.23.cloned.1.call-update) | async-done | bytes 23068688 | tf_op jit(solution)/shard_map/all_gather | solution.py:155
  822.1 15.2 multiply_convert_fusion.1
  837.2 12.3 fusion.99
  849.5 13.9 multiply_reduce_fusion.1
  865.1 11.8 convolution_convert_fusion
  878.1 59.4 %while.30 = (s32[]{:T(128)}, f32[1280,256]{1,0:T(8,128)}, f32[1280,256]{1,0:T(8,128)}, f32[4,32,16,256]{3,2,1,0:T(8,128)}, pred[4,32,1280]{2,1,0:T(8,128)(4,1)S(...) while((s32[]{:T(128)}, f32[1280,256]{1,0:T(8,128)}, ...), condition=%wide.region_15.16_spmd.clone.clone, body=%wide.region_12.15_spmd.clone.sunk.clone | while | flops 1686045952 | bytes 31197332 | solution.py:236
  898.2 3.4 fusion.185
  901.6 3.2 fusion.186
  913.3 3.4 fusion.185
  928.3 3.4 fusion.185
  944.8 9.0 collective-permute-done.5
  955.1 9.2 collective-permute-done.6
  965.7 9.2 collective-permute-done.7
  975.9 23.3 reduce-scatter.10.cloned.1.call-done
  1005.7 6.4 multiply_reduce_fusion.4
  1012.3 4.7 fusion.88
  1017.4 8.3 fusion.84
  1027.2 13.2 fusion.57
  1041.5 19.2 fusion.100
  1060.8 19.2 fusion.101
  1081.0 19.2 fusion.102
  1101.5 12.1 fusion.47
  1116.4 39.9 all-reduce.6
  1159.5 116.3 %reduce-scatter.18.cloned.1.call-done = f32[64,256]{1,0:T(8,128)} async-done(((f32[2048,256]{1,0:T(8,128)}), f32[64,256]{1,0:T(8,128)}) %reduce-scatter.18.cloned.1.call-update) | async-done | bytes 65552 | tf_op jit(solution)/shard_map/reduce_scatter | solution.py:280
  1275.8 182.4 %reduce-scatter.12.cloned.1.call-done = f32[64,1024]{1,0:T(8,128)} async-done(((f32[2048,1024]{1,0:T(8,128)}), f32[64,1024]{1,0:T(8,128)}) %reduce-scatter.12.cloned.1.call-update) | async-done | bytes 262160 | tf_op jit(solution)/shard_map/reduce_scatter | solution.py:277
  1458.3 360.7 %reduce-scatter.14.cloned.1.call-done = f32[32,4096]{1,0:T(8,128)} async-done(((f32[1024,4096]{1,0:T(8,128)}), f32[32,4096]{1,0:T(8,128)}) %reduce-scatter.14.cloned.1.call-update) | async-done | bytes 524304 | tf_op jit(solution)/shard_map/reduce_scatter | solution.py:278
  1819.0 709.9 %reduce-scatter.20.cloned.1.call-done = f32[128,2048]{1,0:T(8,128)} async-done(((f32[4096,2048]{1,0:T(8,128)}), f32[128,2048]{1,0:T(8,128)}) %reduce-scatter.20.cloned.1.call-update) | async-done | bytes 1048592 | tf_op jit(solution)/shard_map/reduce_scatter | solution.py:281
  2528.9 971.5 %reduce-scatter.22.cloned.1.call-done = f32[64,5632]{1,0:T(8,128)} async-done(((f32[2048,5632]{1,0:T(8,128)}), f32[64,5632]{1,0:T(8,128)}) %reduce-scatter.22.cloned.1.call-update) | async-done | bytes 1441808 | tf_op jit(solution)/shard_map/reduce_scatter | solution.py:189
  3500.4 971.2 %reduce-scatter.24.cloned.1.call-done = f32[64,5632]{1,0:T(8,128)} async-done(((f32[2048,5632]{1,0:T(8,128)}), f32[64,5632]{1,0:T(8,128)}) %reduce-scatter.24.cloned.1.call-update) | async-done | bytes 1441808 | tf_op jit(solution)/shard_map/reduce_scatter | solution.py:190
  4471.6 971.2 %reduce-scatter.26.cloned.1.call-done = f32[176,2048]{1,0:T(8,128)} async-done(((f32[5632,2048]{1,0:T(8,128)}), f32[176,2048]{1,0:T(8,128)}) %reduce-scatter.26.cloned.1.call-update) | async-done | bytes 1441808 | tf_op jit(solution)/shard_map/reduce_scatter | solution.py:191
  (281 shorter events, 117.4 us)
Async XLA Ops:
  7.2 140.5 %copy-start = (s32[4096]{0:T(1024)S(1)}, s32[4096]{0:T(1024)}, u32[]{:S(2)}) copy-start(s32[4096]{0:T(1024)} %param.22) | copy-start | bytes 49156
  7.2 48.9 copy-start.2
  7.2 60.2 %all-gather.13.cloned.1.call-start = ((), (), s32[]{:S(2)}) async-start(), calls=%async_computation.11 | async-start | bytes 1081344 | tf_op jit(solution)/shard_map/all_gather | solution.py:105
  8.0 115.1 %all-gather.15.cloned.1.call-start = ((), (), s32[]{:S(2)}) async-start(), calls=%async_computation.12 | async-start | bytes 1081344 | tf_op jit(solution)/shard_map/all_gather | solution.py:106
  8.7 181.1 %all-gather.9.cloned.1.call-start = ((), (), s32[]{:S(2)}) async-start(), calls=%async_computation.9 | async-start | bytes 4325376 | tf_op jit(solution)/shard_map/all_gather | solution.py:103
  9.5 259.3 %all-gather.11.cloned.1.call-start = ((), (), s32[]{:S(2)}) async-start(), calls=%async_computation.10 | async-start | bytes 8650752 | tf_op jit(solution)/shard_map/all_gather | solution.py:104
  10.0 374.9 %all-gather.17.cloned.1.call-start = ((), (), s32[]{:S(2)}) async-start(), calls=%async_computation.13 | async-start | bytes 17301504 | tf_op jit(solution)/shard_map/all_gather | solution.py:107
  10.6 519.9 %all-gather.19.cloned.1.call-start = ((), (), s32[]{:S(2)}) async-start(), calls=%async_computation.14 | async-start | bytes 23789568 | tf_op jit(solution)/shard_map/all_gather | solution.py:153
  11.2 665.1 %all-gather.21.cloned.1.call-start = ((), (), s32[]{:S(2)}) async-start(), calls=%async_computation.15 | async-start | bytes 23789568 | tf_op jit(solution)/shard_map/all_gather | solution.py:154
  12.0 810.1 %all-gather.23.cloned.1.call-start = ((), (), s32[]{:S(2)}) async-start(), calls=%async_computation.16 | async-start | bytes 23789568 | tf_op jit(solution)/shard_map/all_gather | solution.py:155
  12.7 986.4 %reduce-scatter.10.cloned.1.call-start = ((), (), s32[]{:S(2)}) async-start(), calls=%async_computation.17 | async-start | bytes 786432 | tf_op jit(solution)/shard_map/reduce_scatter | solution.py:245
  56.0 133.8 %copy-start.26 = (f32[2048]{0:T(1024)}, f32[2048]{0:T(1024)S(1)}, u32[]{:S(2)}) copy-start(f32[2048]{0:T(1024)S(1)} %convert_element_type.92) | copy-start | bytes 24580
  56.0 75.0 %copy-start.40 = (f32[128]{0:T(128)}, f32[128]{0:T(128)S(1)}, u32[]{:S(2)}) copy-start(f32[128]{0:T(128)S(1)} %multiply_power_fusion) | copy-start | bytes 1540
  56.3 98.5 %copy-start.42 = (f32[128]{0:T(128)}, f32[128]{0:T(128)S(1)}, u32[]{:S(2)}) copy-start(f32[128]{0:T(128)S(1)} %subtract_convert_fusion.3) | copy-start | bytes 1540
  56.8 133.0 %copy-start.36 = (f32[128]{0:T(128)}, f32[128]{0:T(128)S(1)}, u32[]{:S(2)}) copy-start(f32[128]{0:T(128)S(1)} %get-tuple-element.214) | copy-start | bytes 1540
  70.0 204.2 %copy-start.29 = (f32[128,128]{1,0:T(8,128)}, f32[128,128]{1,0:T(8,128)S(1)}, u32[]{:S(2)}) copy-start(f32[128,128]{1,0:T(8,128)S(1)} %get-tuple-element.212) | copy-start | bytes 196612
  131.0 2.5 collective-permute-start
  133.5 7.5 collective-permute-start.1
  141.0 13.8 collective-permute-start.2
  154.8 5.8 collective-permute-start.3
  159.6 109.2 %copy-start.31 = (f32[1024]{0:T(1024)}, f32[1024]{0:T(1024)S(1)}, u32[]{:S(2)}) copy-start(f32[1024]{0:T(1024)S(1)} %convert_element_type.94) | copy-start | bytes 12292
  192.8 80.6 %copy-start.9 = (f32[128,1024]{1,0:T(8,128)}, f32[128,1024]{1,0:T(8,128)S(1)}, u32[]{:S(2)}) copy-start(f32[128,1024]{1,0:T(8,128)S(1)} %get-tuple-element.220) | copy-start | bytes 1572868
  193.4 80.1 %copy-start.38 = (f32[128]{0:T(128)}, f32[128]{0:T(128)S(1)}, u32[]{:S(2)}) copy-start(f32[128]{0:T(128)S(1)} %get-tuple-element.216) | copy-start | bytes 1540
  290.8 94.2 %copy-start.16 = (bf16[4,32,16,256]{3,2,1,0:T(8,128)(2,1)}, bf16[4,32,16,256]{3,2,1,0:T(8,128)(2,1)S(1)}, u32[]{:S(2)}) copy-start(bf16[4,32,16,256]{3,2,1,0:T(8,128)(2,1)S(1)} %get-tuple-element.474) | copy-start | bytes 3145732
  292.9 100.4 %copy-start.13 = (bf16[16,8,16,256]{3,1,2,0:T(8,128)(2,1)}, bf16[16,8,16,256]{3,1,2,0:T(8,128)(2,1)S(1)}, u32[]{:S(2)}) copy-start(bf16[16,8,16,256]{3,1,2,0:T(8,128)(2,1)S(1)} %copy.41) | copy-start | bytes 3145732
  393.2 470.2 %copy-start.4 = (f32[128,2048]{1,0:T(8,128)}, f32[128,2048]{1,0:T(8,128)S(1)}, u32[]{:S(2)}) copy-start(f32[128,2048]{1,0:T(8,128)S(1)} %get-tuple-element.222) | copy-start | bytes 3145732
  393.4 282.9 %copy-start.11 = (bf16[128,2048]{1,0:T(8,128)(2,1)}, bf16[128,2048]{1,0:T(8,128)(2,1)S(1)}, u32[]{:S(2)}) copy-start(bf16[128,2048]{1,0:T(8,128)(2,1)S(1)} %multiply_convert_fusion.4) | copy-start | bytes 1572868
  543.0 279.1 %copy-start.19 = (bf16[128,2048]{1,0:T(8,128)(2,1)S(1)}, bf16[128,2048]{1,0:T(8,128)(2,1)}, u32[]{:S(2)}) copy-start(bf16[128,2048]{1,0:T(8,128)(2,1)} %param.20) | copy-start | bytes 1572868
  849.5 14.0 copy-start.20
  939.4 3.8 collective-permute-start.4
  943.3 55.8 %copy-start.41 = (f32[128]{0:T(128)S(1)}, f32[128]{0:T(128)}, u32[]{:S(2)}) copy-start(f32[128]{0:T(128)} %copy-done.40) | copy-start | bytes 1540
  943.3 55.8 %copy-start.43 = (f32[128]{0:T(128)S(1)}, f32[128]{0:T(128)}, u32[]{:S(2)}) copy-start(f32[128]{0:T(128)} %copy-done.42) | copy-start | bytes 1540
  943.3 57.0 %copy-start.3 = (bf16[128,2048]{1,0:T(8,128)(2,1)S(1)}, bf16[128,2048]{1,0:T(8,128)(2,1)}, u32[]{:S(2)}) copy-start(bf16[128,2048]{1,0:T(8,128)(2,1)} %param.19) | copy-start | bytes 1572868
  943.4 57.0 %copy-start.27 = (f32[2048]{0:T(1024)S(1)}, f32[2048]{0:T(1024)}, u32[]{:S(2)}) copy-start(f32[2048]{0:T(1024)} %copy-done.26) | copy-start | bytes 24580
  943.4 57.0 %copy-start.37 = (f32[128]{0:T(128)S(1)}, f32[128]{0:T(128)}, u32[]{:S(2)}) copy-start(f32[128]{0:T(128)} %copy-done.36) | copy-start | bytes 1540
  943.4 10.4 collective-permute-start.5
  953.8 10.5 collective-permute-start.6
  964.4 10.5 collective-permute-start.7
  975.8 183.7 %reduce-scatter.16.cloned.1.call-start = ((), (), s32[]{:S(2)}) async-start(), calls=%async_computation.20 | async-start | bytes 2162688 | tf_op jit(solution)/shard_map/reduce_scatter | solution.py:279
  1002.4 273.5 %reduce-scatter.18.cloned.1.call-start = ((), (), s32[]{:S(2)}) async-start(), calls=%async_computation.21 | async-start | bytes 2162688 | tf_op jit(solution)/shard_map/reduce_scatter | solution.py:280
  1004.3 453.9 %reduce-scatter.12.cloned.1.call-start = ((), (), s32[]{:S(2)}) async-start(), calls=%async_computation.18 | async-start | bytes 8650752 | tf_op jit(solution)/shard_map/reduce_scatter | solution.py:277
  1017.1 801.9 %reduce-scatter.14.cloned.1.call-start = ((), (), s32[]{:S(2)}) async-start(), calls=%async_computation.19 | async-start | bytes 17301504 | tf_op jit(solution)/shard_map/reduce_scatter | solution.py:278
  1025.7 1503.2 %reduce-scatter.20.cloned.1.call-start = ((), (), s32[]{:S(2)}) async-start(), calls=%async_computation.22 | async-start | bytes 34603008 | tf_op jit(solution)/shard_map/reduce_scatter | solution.py:281
  1040.4 2460.0 %reduce-scatter.22.cloned.1.call-start = ((), (), s32[]{:S(2)}) async-start(), calls=%async_computation.23 | async-start | bytes 47579136 | tf_op jit(solution)/shard_map/reduce_scatter | solution.py:189
  1060.7 3410.9 %reduce-scatter.24.cloned.1.call-start = ((), (), s32[]{:S(2)}) async-start(), calls=%async_computation.24 | async-start | bytes 47579136 | tf_op jit(solution)/shard_map/reduce_scatter | solution.py:190
  1080.0 4362.8 %reduce-scatter.26.cloned.1.call-start = ((), (), s32[]{:S(2)}) async-start(), calls=%async_computation.25 | async-start | bytes 47579136 | tf_op jit(solution)/shard_map/reduce_scatter | solution.py:191
  1115.7 42.3 copy-start.45
  1115.7 4327.1 %copy-start.1 = (s32[4096]{0:T(1024)S(1)}, s32[4096]{0:T(1024)}, u32[]{:S(2)}) copy-start(s32[4096]{0:T(1024)} %param.22) | copy-start | bytes 49156
  (33 other events, 111.3 us)
Sparse Core Ops, SparseCore 0:
  11.0 56.4 all-gather.12
  70.3 52.6 all-gather.14
  126.0 63.7 all-gather.8
  192.7 75.9 all-gather.10
  271.5 113.4 all-gather.16
  387.8 142.7 all-gather.18
  533.5 142.7 all-gather.20
  679.2 142.7 all-gather.22
  975.9 23.1 reduce-scatter.9
  1002.5 137.0 reduce-scatter.15
  1142.4 133.3 reduce-scatter.17
  1278.7 179.5 reduce-scatter.11
  1461.2 357.7 reduce-scatter.13
  1821.8 707.0 reduce-scatter.19
  2531.7 968.6 reduce-scatter.21
  3503.3 968.3 reduce-scatter.23
  4474.5 968.3 reduce-scatter.25
where the time goes:
time: 5460 us; the launch traced here: 5450 us
  waiting for transfers between devices  5010 us (92%)
  matrix products  266 us (5%)
  blocking collectives  88.5 us (2%)
    reduce_scatter x1, waiting for transfers between devices, shards(): lax.psum_scatter(grad_gate, ('blk', 'ctx'), scatter_dimension=0, tiled=True)  972 us
    reduce_scatter x1, waiting for transfers between devices, shards(): lax.psum_scatter(grad_up, ('blk', 'ctx'), scatter_dimension=0, tiled=True)  971 us
    reduce_scatter x1, waiting for transfers between devices, shards(): lax.psum_scatter(grad_down, ('blk', 'ctx'), scatter_dimension=0, tiled=True)  971 us
    reduce_scatter x1, waiting for transfers between devices, shards(): lax.psum_scatter(grad_o, ('blk', 'ctx'), scatter_dimension=0, tiled=True)  710 us
    reduce_scatter x1, waiting for transfers between devices, shards(): lax.psum_scatter(grad_qu, ('blk', 'ctx'), scatter_dimension=0, tiled=True)  361 us
    reduce_scatter x1, waiting for transfers between devices, shards(): lax.psum_scatter(grad_qd, ('blk', 'ctx'), scatter_dimension=0, tiled=True)  182 us
    all_gather x1, waiting for transfers between devices, shards(): lax.all_gather(ffn_parts[1], ('blk', 'ctx'), axis=0, tiled=True)  137 us
    all_gather x1, waiting for transfers between devices, shards(): lax.all_gather(ffn_parts[3], ('blk', 'ctx'), axis=0, tiled=True)  133 us
  transfers between devices with their start and end apart: 25, of which 22 were waited for; matrix products, arithmetic and copies ran while one was open for 3% of the time, Pallas kernels for 0%

commit v1 on v0

v1 whole, which is shorter than its diff:
```python
import jax
import jax.numpy as jnp
from jax import lax
from jax.experimental import pallas as pl
from jax.experimental.pallas import tpu as pltpu
from jax.sharding import Mesh
from jax.sharding import PartitionSpec as P

H = 16
HD = 256
HALF = HD // 2
EPSILON = 1e-06
ROPE_BASE = 10000.0
NEGATIVE = -1e30
LOW = jnp.bfloat16
WIDE = jnp.float32
TILE = 256

ALL = ("r", "x", "c", "y")
PLANE = ("x", "c", "y")


def token_tables(seq_lengths, token_index):
    seq_ends = jnp.cumsum(seq_lengths)
    passed = seq_ends[None, :] <= token_index[:, None]
    return jnp.sum(jnp.where(passed, seq_lengths[None, :], 0), axis=1)


def rope_tables(position):
    frequency = ROPE_BASE ** (-(2.0 * jnp.arange(HALF, dtype=WIDE)) / HD)
    angles = position.astype(WIDE)[:, None] * frequency[None, :]
    return (jnp.cos(angles), jnp.sin(angles))


def rotate(source, cosines, sines):
    first = source[..., :HALF]
    second = source[..., HALF:]
    return jnp.concatenate(
        [first * cosines - second * sines, second * cosines + first * sines], axis=-1
    )


def norm_forward(source, gain_row):
    inv_rms = lax.rsqrt(jnp.mean(source * source, axis=-1, keepdims=True) + EPSILON)
    return (source * inv_rms * gain_row, inv_rms)


def norm_backward(source, inv_rms, gain_row, cotangent):
    weighted = cotangent * gain_row
    d_source = inv_rms * weighted - source * inv_rms**3 * jnp.mean(
        weighted * source, axis=-1, keepdims=True
    )
    d_gain = jnp.sum(cotangent * source * inv_rms, axis=0)
    return (d_source, d_gain)


def dot(left, right, contract):
    return lax.dot_general(left, right, (contract, ((), ())), preferred_element_type=WIDE)


NN = ((1,), (0,))
NT = ((1,), (1,))
TN = ((0,), (0,))


def pick(array, index, axis=0):
    return lax.dynamic_index_in_dim(array, index, axis, keepdims=False)


def across(value, axis, mask):
    count = lax.axis_size(axis)
    return lax.ppermute(value, axis, [(source, source ^ mask) for source in range(count)])


def gathered(value, axes):
    blocks = [value] + [across(value, axes, mask) for mask in range(1, lax.axis_size(axes))]
    return blocks + [across(block, "c", 1) for block in blocks]


def reduced(mine, partners, axes):
    totals = mine + across(partners, "c", 1).astype(WIDE)
    result = totals[0]
    for mask in range(1, totals.shape[0]):
        result = result + across(totals[mask].astype(LOW), axes, mask).astype(WIDE)
    return result


def summed_over(parts, index, axes):
    result = pick(parts, index)
    for mask in range(1, lax.axis_size(axes)):
        sent = pick(parts, index ^ mask).astype(LOW)
        result = result + across(sent, axes, mask).astype(WIDE)
    return result


def visible_of(q_index, q_start, k_index, k_live):
    return ((k_live >= q_start) & (k_live <= q_index)) | (k_index == q_index)


def twice(value):
    return jnp.concatenate([value, value], axis=0)


def stacked(ref):
    return jnp.concatenate([ref[:, :HD], ref[:, HD:]], axis=0)


def attend_kernel(
    count, ids, q_ref, k_ref, v_ref, qi_ref, qs_ref, ki_ref, kl_ref, o_ref, lse_ref, s_ref, acc_ref
):
    step = pl.program_id(0)
    tiles = k_ref.shape[0] // TILE
    total = count[step]
    queries = stacked(q_ref)
    q_index, q_start = twice(qi_ref[...]), twice(qs_ref[...])

    def score(turn, row_max):
        tile = ids[step * tiles + turn]
        keys = k_ref[pl.ds(pl.multiple_of(tile * TILE, TILE), TILE), :]
        seen = visible_of(q_index, q_start, ki_ref[tile], kl_ref[tile])
        scores = jnp.where(seen, dot(queries, keys, NT) * (HD**-0.5), NEGATIVE)
        s_ref[turn] = scores
        return jnp.maximum(row_max, jnp.max(scores, axis=1, keepdims=True))

    row_max = lax.fori_loop(0, total, score, jnp.full((2 * TILE, 1), NEGATIVE, WIDE))
    acc_ref[...] = jnp.zeros_like(acc_ref)

    def attend(turn, denominator):
        tile = ids[step * tiles + turn]
        probs = jnp.exp(s_ref[turn] - row_max)
        values = v_ref[pl.ds(pl.multiple_of(tile * TILE, TILE), TILE), :]
        acc_ref[...] += dot(probs.astype(LOW), values, NN)
        return denominator + jnp.sum(probs, axis=1, keepdims=True)

    denominator = lax.fori_loop(0, total, attend, jnp.zeros((2 * TILE, 1), WIDE))
    result = (acc_ref[...] / denominator).astype(LOW)
    log_total = row_max + jnp.log(denominator)
    for head in range(2):
        rows = slice(head * TILE, (head + 1) * TILE)
        o_ref[:, head * HD : (head + 1) * HD] = result[rows]
        lse_ref[:, head : head + 1] = log_total[rows]


def attend_back_kernel(
    count,
    ids,
    q_ref,
    k_ref,
    v_ref,
    qi_ref,
    qs_ref,
    ki_ref,
    kl_ref,
    o_ref,
    do_ref,
    lse_ref,
    cos_ref,
    sin_ref,
    dq_ref,
    dk_ref,
    dv_ref,
    acc_ref,
):
    step = pl.program_id(0)
    tiles = k_ref.shape[0] // TILE

    @pl.when(step == 0)
    def _():
        dk_ref[...] = jnp.zeros_like(dk_ref)
        dv_ref[...] = jnp.zeros_like(dv_ref)

    queries, d_out = stacked(q_ref), stacked(do_ref)
    q_index, q_start = twice(qi_ref[...]), twice(qs_ref[...])
    log_total = jnp.concatenate([lse_ref[:, 0:1], lse_ref[:, 1:2]], axis=0)
    delta = jnp.sum(d_out.astype(WIDE) * stacked(o_ref).astype(WIDE), axis=1, keepdims=True)
    acc_ref[...] = jnp.zeros_like(acc_ref)
    scale = HD**-0.5

    def back(turn, unused):
        tile = ids[step * tiles + turn]
        rows = pl.ds(pl.multiple_of(tile * TILE, TILE), TILE)
        keys, values = k_ref[rows, :], v_ref[rows, :]
        seen = visible_of(q_index, q_start, ki_ref[tile], kl_ref[tile])
        scores = jnp.where(seen, dot(queries, keys, NT) * scale, NEGATIVE)
        soft = jnp.exp(scores - log_total)
        d_probs = dot(d_out, values, NT)
        d_scores = (soft * (d_probs - delta)).astype(LOW)
        dv_ref[rows, :] += dot(soft.astype(LOW), d_out, TN)
        dk_ref[rows, :] += dot(d_scores, queries, TN) * scale
        acc_ref[...] += dot(d_scores, keys, NN)
        return unused

    lax.fori_loop(0, count[step], back, 0)
    cosines, sines = cos_ref[...], sin_ref[...]
    for head in range(2):
        d_query = acc_ref[head * TILE : (head + 1) * TILE, :] * scale
        turned = rotate(d_query, cosines, -sines)
        dq_ref[:, head * HD : (head + 1) * HD] = turned.astype(LOW)


def by_query(width):
    return pl.BlockSpec((TILE, width), lambda i, *unused: (i, 0))


def whole(shape):
    return pl.BlockSpec(shape, lambda i, *unused: (0,) * len(shape))


def attend(count, ids, queries, keys, values, q_index, q_start, k_index, k_live):
    rows, span = queries.shape[0], keys.shape[0]
    tiles = span // TILE
    return pl.pallas_call(
        attend_kernel,
        grid_spec=pltpu.PrefetchScalarGridSpec(
            num_scalar_prefetch=2,
            grid=(rows // TILE,),
            in_specs=[
                by_query(2 * HD),
                whole((span, HD)),
                whole((span, HD)),
                by_query(1),
                by_query(1),
                whole((tiles, 1, TILE)),
                whole((tiles, 1, TILE)),
            ],
            out_specs=[by_query(2 * HD), by_query(2)],
            scratch_shapes=[
                pltpu.VMEM((tiles, 2 * TILE, TILE), WIDE),
                pltpu.VMEM((2 * TILE, HD), WIDE),
            ],
        ),
        out_shape=[
            jax.ShapeDtypeStruct((rows, 2 * HD), LOW),
            jax.ShapeDtypeStruct((rows, 2), WIDE),
        ],
        compiler_params=pltpu.CompilerParams(vmem_limit_bytes=40 * 2**20),
        cost_estimate=pl.CostEstimate(
            flops=4 * 2 * rows * 5 * TILE * HD, bytes_accessed=6 * 2**20, transcendentals=rows * 2560
        ),
        name="attend",
    )(count, ids, queries, keys, values, q_index, q_start, k_index, k_live)


def attend_back(
    count, ids, queries, keys, values, q_index, q_start, k_index, k_live, attended, d_out, lse, cosines, sines
):
    rows, span = queries.shape[0], keys.shape[0]
    tiles = span // TILE
    return pl.pallas_call(
        attend_back_kernel,
        grid_spec=pltpu.PrefetchScalarGridSpec(
            num_scalar_prefetch=2,
            grid=(rows // TILE,),
            in_specs=[
                by_query(2 * HD),
                whole((span, HD)),
                whole((span, HD)),
                by_query(1),
                by_query(1),
                whole((tiles, 1, TILE)),
                whole((tiles, 1, TILE)),
                by_query(2 * HD),
                by_query(2 * HD),
                by_query(2),
                by_query(HALF),
                by_query(HALF),
            ],
            out_specs=[by_query(2 * HD), whole((span, HD)), whole((span, HD))],
            scratch_shapes=[pltpu.VMEM((2 * TILE, HD), WIDE)],
        ),
        out_shape=[
            jax.ShapeDtypeStruct((rows, 2 * HD), LOW),
            jax.ShapeDtypeStruct((span, HD), WIDE),
            jax.ShapeDtypeStruct((span, HD), WIDE),
        ],
        compiler_params=pltpu.CompilerParams(vmem_limit_bytes=40 * 2**20),
        cost_estimate=pl.CostEstimate(
            flops=10 * 2 * rows * 5 * TILE * HD, bytes_accessed=12 * 2**20, transcendentals=rows * 2560
        ),
        name="attend_back",
    )(count, ids, queries, keys, values, q_index, q_start, k_index, k_live, attended, d_out, lse, cosines, sines)


def slot_order(array, x, c, y):
    for axis, bit in ((0, x), (1, c), (2, y)):
        array = jnp.where(bit == 1, jnp.flip(array, axis), array)
    moved = jnp.transpose(array, (1, 0, 2) + tuple(range(3, array.ndim)))
    return moved.reshape((8,) + array.shape[3:])


def o_rows_for_heads(o_proj, planes, x, c, y):
    if planes == 4:
        lines = lax.all_gather(o_proj, "r", axis=0).reshape((2, 2) + o_proj.shape)
        keep, send = pick(lines, y), pick(lines, 1 - y)
        received = across(send, "y", 1)
        low_half = jnp.where(y == 0, keep, received)
        high_half = jnp.where(y == 0, received, keep)
        return jnp.stack([low_half, high_half], axis=1).reshape(2 * HD, -1)
    full = lax.all_gather(o_proj, ALL, axis=0, tiled=True)
    heads = full.reshape(2, 2, 2, 2, HD, full.shape[1])
    return pick(pick(pick(heads, y), x, 1), c, 1).reshape(2 * HD, -1)


def o_grad_to_owner(grad, planes, r, x, c, y):
    width = grad.shape[1]
    if planes == 4:
        halves = grad.reshape(2, 2, HALF, width)
        keep = pick(halves, y, 1).astype(LOW)
        received = across(pick(halves, 1 - y, 1).astype(LOW), "y", 1)
        lines = jnp.concatenate(
            [jnp.where(y == 0, keep, received), jnp.where(y == 0, received, keep)], axis=0
        )
        return summed_over(lines, r, "r").astype(WIDE)
    place = jnp.zeros((2, 2, 2, 2, HD, width), WIDE)
    place = lax.dynamic_update_slice(
        place, grad.reshape(1, 2, 1, 1, HD, width), (y, 0, x, c, 0, 0)
    ).reshape(H * HD, width)
    return lax.psum_scatter(place, ALL, scatter_dimension=0, tiled=True)


def gains_to_owner(grads, r, x, c, y):
    kept = pick(grads, c, 2) + across(pick(grads, 1 - c, 2), "c", 1)
    kept = kept.reshape(kept.shape[0], 4, kept.shape[-1])
    place = x * 2 + y
    total = pick(kept, place, 1)
    for mask in range(1, 4):
        total = total + across(pick(kept, place ^ mask, 1), ("x", "y"), mask)
    result = pick(total, r)
    for mask in range(1, total.shape[0]):
        result = result + across(pick(total, r ^ mask), "r", mask)
    return result


def shards(
    inputs,
    out_grad,
    seq_lengths,
    key_live,
    attn_gain,
    q_down,
    q_gain,
    q_up,
    k_proj,
    v_proj,
    o_proj,
    ffn_gain,
    w_gate,
    w_up,
    w_down,
):
    rows, width = inputs.shape
    planes = lax.axis_size("r")
    r, x, c, y = (lax.axis_index(axis) for axis in ALL)
    place = x * 2 + y
    plane_rows = 8 * rows
    latent_width = q_down.shape[1]
    hidden_part = w_down.shape[0]
    hidden_width = 4 * hidden_part
    gate_rows = w_gate.shape[0]

    gains = lax.all_gather(jnp.concatenate([attn_gain, ffn_gain, q_gain]), ALL, axis=0).astype(WIDE)
    n_attn, n_ffn = attn_gain.shape[0], ffn_gain.shape[0]
    gain_attn = gains[:, :n_attn].reshape(1, -1)
    gain_ffn = gains[:, n_attn : n_attn + n_ffn].reshape(1, -1)
    gain_query = gains[:, n_attn + n_ffn :].reshape(1, -1)

    full_down = lax.all_gather(
        jnp.concatenate([q_down, k_proj, v_proj], axis=1), ALL, axis=0, tiled=True
    )

    up_rows = q_up.shape[0]
    q_up_sent = jnp.transpose(q_up.reshape(up_rows, 2, 2, 2, 2, HD), (3, 4, 1, 0, 2, 5))
    q_up_plane = lax.all_to_all(
        q_up_sent.reshape(8, up_rows, 2 * HD), PLANE, split_axis=0, concat_axis=0, tiled=True
    )
    q_up_heads = lax.all_gather(q_up_plane, "r", axis=0).reshape(latent_width, 2 * HD)
    o_heads = o_rows_for_heads(o_proj, planes, x, c, y)

    gate_up = jnp.stack([w_gate, w_up]).reshape(2, gate_rows, planes, 2, 2, 2, hidden_part)
    gate_up = jnp.transpose(gate_up, (0, 2, 4, 1, 3, 5, 6)).reshape(
        2, planes * 2, gate_rows, hidden_width
    )
    gate_up = lax.all_to_all(gate_up, ("r", "c"), split_axis=1, concat_axis=1, tiled=True)
    down_hidden = lax.all_gather(w_down, ("x", "y"), axis=0, tiled=True)
    gate_up = lax.all_gather(gate_up, ("x", "y"), axis=0)
    gate_up = jnp.transpose(
        gate_up.reshape(2, 2, 2, planes, 2, gate_rows, hidden_width), (2, 3, 0, 4, 1, 5, 6)
    ).reshape(2, width, hidden_width)
    gate_hidden, up_hidden = gate_up[0], gate_up[1]

    slots = jnp.arange(8, dtype=jnp.int32)
    slot_place = (
        ((slots // 2 % 2) ^ x) * 4 + ((slots // 4) ^ c) * 2 + ((slots % 2) ^ y)
    )
    within = slot_place[:, None] * rows + jnp.arange(rows, dtype=jnp.int32)[None, :]
    q_index = (r * plane_rows + within).reshape(plane_rows)
    q_start = token_tables(seq_lengths, q_index)
    cosines, sines = rope_tables(q_index - q_start)
    k_index = jnp.concatenate([q_index, q_index - plane_rows])
    live = jnp.concatenate([jnp.zeros((plane_rows,), jnp.int32), key_live])
    live = lax.dynamic_slice_in_dim(live, r * plane_rows, 2 * plane_rows)
    live = live.reshape(2, 2, 2, 2, rows)
    live = jnp.concatenate(
        [slot_order(live[1], x, c, y).reshape(-1), slot_order(live[0], x, c, y).reshape(-1)]
    )
    k_live = jnp.where(live == 1, k_index, -1)
    q_tiles, k_tiles = plane_rows // TILE, 2 * plane_rows // TILE
    q_tile, k_tile = q_index.reshape(q_tiles, TILE), k_index.reshape(k_tiles, TILE)
    needed = (
        jnp.max(k_tile, axis=1)[None, :] >= jnp.min(q_start.reshape(q_tiles, TILE), axis=1)[:, None]
    ) & (jnp.min(k_tile, axis=1)[None, :] <= jnp.max(q_tile, axis=1)[:, None])
    needed = needed.astype(jnp.int32)
    turn = jnp.cumsum(needed, axis=1) - 1
    chosen = (turn[:, None, :] == jnp.arange(k_tiles)[None, :, None]) & (needed[:, None, :] == 1)
    ids = jnp.sum(jnp.where(chosen, jnp.arange(k_tiles)[None, None, :], 0), axis=2)
    ids = ids.astype(jnp.int32).reshape(-1)
    count = jnp.sum(needed, axis=1).astype(jnp.int32)
    tables = (
        q_index[:, None],
        q_start[:, None],
        k_index.reshape(k_tiles, 1, TILE),
        k_live.reshape(k_tiles, 1, TILE),
    )

    out_grads = jnp.concatenate(gathered(out_grad, "r"), axis=0)

    x_float = inputs.astype(WIDE)
    normed_float, x_inv = norm_forward(x_float, gain_attn)
    normed = normed_float.astype(LOW)
    low = dot(normed, full_down, NN)
    latent = low[:, :latent_width]
    latent_float, latent_inv = norm_forward(latent, gain_query)
    key_rows = rotate(low[:, latent_width : latent_width + HD], cosines[:rows], sines[:rows])
    values = low[:, latent_width + HD :]
    own = jnp.concatenate([latent_float, key_rows, values], axis=1).astype(LOW)
    earlier = lax.ppermute(
        own[:, latent_width:], "r", [(source, source + 1) for source in range(planes - 1)]
    )
    plane = jnp.concatenate(gathered(jnp.concatenate([own, earlier], axis=1), ("x", "y")), axis=0)
    latents = plane[:, :latent_width]
    at = latent_width
    win_keys = jnp.concatenate([plane[:, at : at + HD], plane[:, at + 2 * HD : at + 3 * HD]])
    win_values = jnp.concatenate([plane[:, at + HD : at + 2 * HD], plane[:, at + 3 * HD :]])
    q_pre = dot(latents, q_up_heads, NN)
    queries = jnp.concatenate(
        [rotate(q_pre[:, :HD], cosines, sines), rotate(q_pre[:, HD:], cosines, sines)], axis=1
    ).astype(LOW)
    attended, log_total = attend(count, ids, queries, win_keys, win_values, *tables)
    o_mine = dot(attended[: plane_rows // 2], o_heads, NN).reshape(4, rows, width)
    o_partner = dot(attended[plane_rows // 2 :], o_heads, NN).astype(LOW).reshape(4, rows, width)
    middle = x_float + reduced(o_mine, o_partner, ("x", "y"))

    mid_float, mid_inv = norm_forward(middle, gain_ffn)
    normed_mid = jnp.concatenate(gathered(mid_float.astype(LOW), "r"), axis=0)
    gate_act = dot(normed_mid, gate_hidden, NN)
    up_act = dot(normed_mid, up_hidden, NN)
    sigmoid_gate = jax.nn.sigmoid(gate_act)
    silu_gate = gate_act * sigmoid_gate
    hidden = (silu_gate * up_act).astype(LOW)
    d_hidden = dot(out_grads, down_hidden, NT)
    d_gate = (d_hidden * up_act * sigmoid_gate * (1.0 + gate_act * (1.0 - sigmoid_gate))).astype(LOW)
    d_up = (d_hidden * silu_gate).astype(LOW)
    half = planes * rows

    def d_normed_of(part):
        return dot(d_gate[part], gate_hidden, NT) + dot(d_up[part], up_hidden, NT)

    d_partner = d_normed_of(slice(half, None)).astype(LOW).reshape(planes, rows, width)
    d_mine = d_normed_of(slice(0, half)).reshape(planes, rows, width)
    d_normed_mid = reduced(d_mine, d_partner, "r")
    out_partner = dot(hidden[half:], down_hidden, NN).astype(LOW).reshape(planes, rows, width)
    out_mine = dot(hidden[:half], down_hidden, NN).reshape(planes, rows, width)
    output = (middle + reduced(out_mine, out_partner, "r")).astype(LOW)
    grad_down = dot(hidden, out_grads, TN).reshape(4, hidden_part, width)
    grad_down = summed_over(grad_down, place, ("x", "y"))

    def rows_by_place(grad):
        grad = grad.reshape(planes, 2, 2, 2, gate_rows, hidden_width)
        return jnp.transpose(grad, (1, 3, 0, 2, 4, 5)).reshape(
            4, planes * 2, gate_rows, hidden_width
        )

    grad_gate_up = jnp.stack(
        [
            rows_by_place(dot(normed_mid, d_gate, TN)),
            rows_by_place(dot(normed_mid, d_up, TN)),
        ],
        axis=1,
    )
    grad_gate_up = summed_over(grad_gate_up, place, ("x", "y")).astype(LOW)
    grad_gate_up = lax.all_to_all(grad_gate_up, ("r", "c"), split_axis=1, concat_axis=1, tiled=True)
    grad_gate_up = jnp.transpose(
        grad_gate_up.reshape(2, planes, 2, gate_rows, 2, 2, hidden_part), (0, 3, 1, 4, 2, 5, 6)
    ).reshape(2, gate_rows, -1)
    grad_gate_up = grad_gate_up.astype(WIDE)

    d_mid_norm, grad_gain_ffn = norm_backward(middle, mid_inv, gain_ffn, d_normed_mid)
    d_middle = out_grad.astype(WIDE) + d_mid_norm
    d_middles = jnp.concatenate(gathered(d_middle.astype(LOW), ("x", "y")), axis=0)
    d_attended = dot(d_middles, o_heads, NT).astype(LOW)
    grad_o = o_grad_to_owner(dot(attended, d_middles, TN), planes, r, x, c, y)
    dq_low, d_win_keys, d_win_values = attend_back(
        count,
        ids,
        queries,
        win_keys,
        win_values,
        *tables,
        attended,
        d_attended,
        log_total,
        cosines,
        sines,
    )
    d_latents = dot(dq_low, q_up_heads, NT)
    terms = jnp.concatenate(
        [
            d_latents,
            d_win_keys[:plane_rows],
            d_win_values[:plane_rows],
            d_win_keys[plane_rows:],
            d_win_values[plane_rows:],
        ],
        axis=1,
    ).reshape(2, 4, rows, -1)
    summed = reduced(terms[0], terms[1].astype(LOW), ("x", "y"))
    later = lax.ppermute(
        summed[:, latent_width + 2 * HD :].astype(LOW),
        "r",
        [(source, source - 1) for source in range(1, planes)],
    ).astype(WIDE)
    own_grads = summed[:, latent_width : latent_width + 2 * HD] + later
    dk_low = rotate(own_grads[:, :HD], cosines[:rows], -sines[:rows]).astype(LOW)
    dv_low = own_grads[:, HD:].astype(LOW)
    grad_q_up = dot(latents, dq_low, TN).reshape(planes, 8, up_rows, 2 * HD)
    grad_q_up = summed_over(grad_q_up, r, "r").astype(LOW)
    grad_q_up = lax.all_to_all(grad_q_up, PLANE, split_axis=0, concat_axis=0, tiled=True)
    grad_q_up = jnp.transpose(
        grad_q_up.reshape(2, 2, 2, up_rows, 2, HD), (3, 2, 4, 0, 1, 5)
    ).reshape(up_rows, -1)
    grad_q_up = grad_q_up.astype(WIDE)

    d_latent, grad_gain_query = norm_backward(
        latent, latent_inv, gain_query, summed[:, :latent_width]
    )
    d_low = jnp.concatenate([d_latent.astype(LOW), dk_low, dv_low], axis=1)
    d_lows = lax.all_gather(d_low, PLANE, axis=0, tiled=True)
    columns = jnp.transpose(
        normed.reshape(rows, planes, 8, gate_rows), (2, 0, 1, 3)
    ).reshape(8, rows, planes * gate_rows)
    columns = lax.all_to_all(columns, PLANE, split_axis=0, concat_axis=0, tiled=True)
    grad_low = dot(columns.reshape(plane_rows, -1), d_lows, TN).reshape(planes, gate_rows, -1)
    grad_low = summed_over(grad_low, r, "r")
    d_normed = dot(d_low, full_down, NT)
    d_x_norm, grad_gain_attn = norm_backward(x_float, x_inv, gain_attn, d_normed)
    input_grad = d_middle + d_x_norm
    grad_gains = jnp.concatenate(
        [
            grad_gain_attn.reshape(planes, 2, 2, 2, -1),
            grad_gain_ffn.reshape(planes, 2, 2, 2, -1),
            grad_gain_query.reshape(planes, 2, 2, 2, -1),
        ],
        axis=-1,
    )
    grad_gains = gains_to_owner(grad_gains, r, x, c, y)
    return (
        output,
        input_grad,
        grad_gains[:n_attn],
        grad_low[:, :latent_width],
        grad_gains[n_attn + n_ffn :],
        grad_q_up,
        grad_low[:, latent_width : latent_width + HD],
        grad_low[:, latent_width + HD :],
        grad_o,
        grad_gains[n_attn : n_attn + n_ffn],
        grad_gate_up[0],
        grad_gate_up[1],
        grad_down,
    )


def solution(mesh):
    devices = mesh.devices.reshape(-1, 2, 2, 2)
    grid = Mesh(devices, ALL)
    split, split_rows = P(ALL), P(ALL, None)
    placed = (split_rows, split_rows, P(), P(), split, split_rows, split) + (split_rows,) * 4 + (
        split,
    ) + (split_rows,) * 3
    return jax.shard_map(
        shards,
        mesh=grid,
        in_specs=placed,
        out_specs=(
            (split_rows, split_rows, split, split_rows, split)
            + (split_rows,) * 4
            + (split,)
            + (split_rows,) * 3
        ),
        check_vma=False,
    )
```

time: 5460 us -> 894 us (0.16)
  waiting for transfers between devices: 5010 us -> 404 us
  matrix products: 266 us -> 82.2 us
  local copies, waits for them, and re-layouts: 26.4 us -> 139 us
  starting transfers between devices: 25.1 us -> 123 us
    reduce_scatter x9 -> x0, waiting for transfers between devices: 4310 us -> none  [the longest x1 972 us: shards(): lax.psum_scatter(grad_gate, ('blk', 'ctx'), scatter_dimension=0, tiled=True)]
    all_gather x8 -> x6, waiting for transfers between devices: 663 us -> 0.03 us  [the longest x1 0.02 us: o_rows_for_heads(): lines = lax.all_gather(o_proj, 'r', axis=0).reshape((2, 2) + o_proj.shape)]
    ppermute x8 -> x70, waiting for transfers between devices: 32 us -> 336 us  [the longest x68 325 us: across(): lax.ppermute(value, axis, [(source, source ^ mask) for source in range(co...]
    dot_general x52 -> x22, matrix products: 266 us -> 82.2 us  [dot(): lax.dot_general(left, right, (contract, ((), ())), preferred_element_type...]
    ppermute x8 -> x70, starting transfers between devices: 24 us -> 101 us  [the longest x68 98.7 us: across(): lax.ppermute(value, axis, [(source, source ^ mask) for source in range(co...]
    all_to_all x0 -> x5, waiting for transfers between devices: none -> 66.9 us  [the longest x1 58.1 us: shards(): lax.all_to_all(gate_up, ('r', 'c'), split_axis=1, concat_axis=1, tiled=True)]
  transfers between devices with their start and end apart: 25 -> 81, of which waited for: 22 -> 31; matrix products, arithmetic and copies ran while one was open for 3% -> 25% of each run, Pallas kernels for 0% -> 1%
where the time goes in v1:
time: 894 us; the launch traced here: 885 us
  waiting for transfers between devices  404 us (45%)
  local copies, waits for them, and re-layouts  139 us (16%)
  starting transfers between devices  123 us (14%)
  matrix products  82.2 us (9%)
  other arithmetic  60.5 us (7%)
  blocking collectives  44.4 us (5%)
  between operations  16.3 us (2%)
  Pallas kernels  15.3 us (2%)
    ppermute x68, waiting for transfers between devices, across(): lax.ppermute(value, axis, [(source, source ^ mask) for source in range(co...  325 us
    ppermute x68, starting transfers between devices, across(): lax.ppermute(value, axis, [(source, source ^ mask) for source in range(co...  98.7 us
    dot_general x22, matrix products, dot(): lax.dot_general(left, right, (contract, ((), ())), preferred_element_type...  82.2 us
    all_to_all x1, waiting for transfers between devices, shards(): lax.all_to_all(gate_up, ('r', 'c'), split_axis=1, concat_axis=1, tiled=True)  58.1 us
    unnamed x1, blocking collectives  44.4 us
    unnamed x206, local copies, waits for them, and re-layouts  33.2 us
  transfers between devices with their start and end apart: 81, of which 31 were waited for; matrix products, arithmetic and copies ran while one was open for 25% of the time, Pallas kernels for 1%

profile of v1, /device:TPU:0, one launch (start us, length us, event | category | flops | bytes accessed | tf_op | source)
XLA Modules:
  0.0 884.6 jit_solution(5481582186962876442)
XLA Ops:
  11.9 5.2 all-to-all-start
  18.7 44.4 %all-reduce.1 = bf16[5120]{0:T(1024)(128)(2,1)S(1)} all-reduce(bf16[5120]{0:T(1024)(128)(2,1)S(1)} %dynamic-update-slice), channel_id=2, replica_groups=mesh['r'=4,'x'=2,'c'=2,'y'=2] {'r','x','c','y'}, use_global_device_ids=true, to_apply=%add.1 | all-reduce | flops 5120 | bytes 20480
  71.5 7.5 reshape.672
  81.8 4.3 all-to-all-start.1
  90.2 58.1 %all-to-all-done.1 = bf16[2,8,64,704]{3,2,0,1:T(8,128)(2,1)} async-done(((bf16[2,8,64,704]{3,2,0,1:T(8,128)(2,1)}), bf16[2,8,64,704]{3,2,0,1:T(8,128)(2,1)}, u32[]{:S(2)}, u32[]{:S(2)}) %all-to-all-start.1) | async-done | bytes 1441824 | tf_op jit(solution)/shard_map/all_to_all | solution.py:383
  164.0 5.0 collective-permute-done
  171.7 8.5 collective-permute-done.8
  185.5 23.3 %collective-permute-done.1 = bf16[128,2048]{1,0:T(8,128)(2,1)S(1)} collective-permute-done((bf16[128,2048]{1,0:T(8,128)(2,1)S(1)}, bf16[128,2048]{1,0:T(8,128)(2,1)S(1)}, u32[]{:S(2)}, u32[]{:S(2)}) %collective-permute-start.1) | collective-permute-done | bytes 524320 | tf_op jit(solution)/shard_map/ppermute | solution.py:72
  222.8 6.9 attend.1
  238.2 18.5 %collective-permute-done.24 = bf16[128,2048]{1,0:T(8,128)(2,1)} collective-permute-done((bf16[128,2048]{1,0:T(8,128)(2,1)S(1)}, bf16[128,2048]{1,0:T(8,128)(2,1)}, u32[]{:S(2)}, u32[]{:S(2)}) %collective-permute-start.24) | collective-permute-done | bytes 524320 | tf_op jit(solution)/shard_map/ppermute | solution.py:72
  256.7 14.5 %collective-permute-done.25 = bf16[128,2048]{1,0:T(8,128)(2,1)} collective-permute-done((bf16[128,2048]{1,0:T(8,128)(2,1)S(1)}, bf16[128,2048]{1,0:T(8,128)(2,1)}, u32[]{:S(2)}, u32[]{:S(2)}) %collective-permute-start.25) | collective-permute-done | bytes 524320 | tf_op jit(solution)/shard_map/ppermute | solution.py:72
  287.5 15.4 %collective-permute-done.12 = bf16[128,2048]{1,0:T(8,128)(2,1)S(1)} collective-permute-done((bf16[128,2048]{1,0:T(8,128)(2,1)S(1)}, bf16[128,2048]{1,0:T(8,128)(2,1)S(1)}, u32[]{:S(2)}, u32[]{:S(2)}) %collective-permute-start.12) | collective-permute-done | bytes 524320 | tf_op jit(solution)/shard_map/ppermute | solution.py:72
  303.0 20.0 %collective-permute-done.11 = bf16[128,2048]{1,0:T(8,128)(2,1)S(1)} collective-permute-done((bf16[128,2048]{1,0:T(8,128)(2,1)S(1)}, bf16[128,2048]{1,0:T(8,128)(2,1)S(1)}, u32[]{:S(2)}, u32[]{:S(2)}) %collective-permute-start.11) | collective-permute-done | bytes 524320 | tf_op jit(solution)/shard_map/ppermute | solution.py:72
  335.0 11.5 %collective-permute-done.13 = bf16[128,2048]{1,0:T(8,128)(2,1)S(1)} collective-permute-done((bf16[128,2048]{1,0:T(8,128)(2,1)S(1)}, bf16[128,2048]{1,0:T(8,128)(2,1)S(1)}, u32[]{:S(2)}, u32[]{:S(2)}) %collective-permute-start.13) | collective-permute-done | bytes 524320 | tf_op jit(solution)/shard_map/ppermute | solution.py:72
  346.6 23.7 %collective-permute-done.14 = bf16[128,2048]{1,0:T(8,128)(2,1)S(1)} collective-permute-done((bf16[128,2048]{1,0:T(8,128)(2,1)S(1)}, bf16[128,2048]{1,0:T(8,128)(2,1)S(1)}, u32[]{:S(2)}, u32[]{:S(2)}) %collective-permute-start.14) | collective-permute-done | bytes 524320 | tf_op jit(solution)/shard_map/ppermute | solution.py:72
  372.9 5.0 fusion.152
  377.9 5.1 fusion.153
  383.0 9.0 %multiply_convert_fusion = (bf16[1024,704]{0,1:T(8,128)(2,1)S(1)}, bf16[1024,704]{0,1:T(8,128)(2,1)S(1)}, bf16[1024,704]{0,1:T(8,128)(2,1)S(1)}) fusion(f32[1024,704]{0,1:T(8,128)} %fusion.152, f32[1024,704]{0,1:T(8,128)} %fusion.153, bf16[1024,2048]{1,0:T(8,128)(2,1)} %constant_dynamic-update-slice_fusion.25, ...), kind=kOutput, calls=%fused_computation.42 | convolution fusion | flops 2963603456 | bytes 17170432 | tf_op jit(solution)/shard_map/dot_general | solution.py:58
  412.4 8.5 collective-permute-start.33
  429.4 21.1 %collective-permute-start.21 = (bf16[128,2048]{1,0:T(8,128)(2,1)}, bf16[128,2048]{1,0:T(8,128)(2,1)}, u32[]{:S(2)}, u32[]{:S(2)}) collective-permute-start(bf16[128,2048]{1,0:T(8,128)(2,1)} %get-tuple-element.98), channel_id=1, source_target_pairs={{0,8},{8,0},{16,24},{24,16},{1,9},{9,1},{17,25},{25,17},{2,10},{10... | collective-permute-start | bytes 1572872 | tf_op jit(solution)/shard_map/ppermute | solution.py:72
  455.3 8.7 all-to-all-done.2
  465.2 16.9 %collective-permute-done.33 = bf16[128,2048]{1,0:T(8,128)(2,1)} collective-permute-done((bf16[128,2048]{1,0:T(8,128)(2,1)}, bf16[128,2048]{1,0:T(8,128)(2,1)}, u32[]{:S(2)}, u32[]{:S(2)}) %collective-permute-start.33) | collective-permute-done | bytes 524320 | tf_op jit(solution)/shard_map/ppermute | solution.py:72
  482.2 22.4 %collective-permute-done.22 = bf16[128,2048]{1,0:T(8,128)(2,1)} collective-permute-done((bf16[128,2048]{1,0:T(8,128)(2,1)}, bf16[128,2048]{1,0:T(8,128)(2,1)}, u32[]{:S(2)}, u32[]{:S(2)}) %collective-permute-start.22) | collective-permute-done | bytes 524320 | tf_op jit(solution)/shard_map/ppermute | solution.py:72
  504.6 4.3 multiply_reduce_fusion
  527.6 9.1 %collective-permute-done.37 = bf16[128,2048]{1,0:T(8,128)(2,1)S(1)} collective-permute-done((bf16[128,2048]{1,0:T(8,128)(2,1)S(1)}, bf16[128,2048]{1,0:T(8,128)(2,1)S(1)}, u32[]{:S(2)}, u32[]{:S(2)}) %collective-permute-start.37) | collective-permute-done | bytes 524320 | tf_op jit(solution)/shard_map/ppermute | solution.py:72
  541.0 4.7 convolution_convert_fusion.2.do_ref
  545.8 8.4 attend_back.1
  577.5 5.7 fusion.156
  594.6 5.2 fusion.157
  605.5 5.5 copy.181
  612.5 6.2 fusion.137
  620.0 9.7 %collective-permute-done.66 = bf16[2,8,64,704]{3,2,1,0:T(8,128)(2,1)} collective-permute-done((bf16[2,8,64,704]{3,2,1,0:T(8,128)(2,1)}, bf16[2,8,64,704]{3,2,1,0:T(8,128)(2,1)}, u32[]{:S(2)}, u32[]{:S(2)}) %collective-permute-start.66) | collective-permute-done | bytes 1441824 | tf_op jit(solution)/shard_map/ppermute | solution.py:72
  631.1 32.3 %collective-permute-done.65 = bf16[2,8,64,704]{3,2,1,0:T(8,128)(2,1)} collective-permute-done((bf16[2,8,64,704]{3,2,1,0:T(8,128)(2,1)}, bf16[2,8,64,704]{3,2,1,0:T(8,128)(2,1)}, u32[]{:S(2)}, u32[]{:S(2)}) %collective-permute-start.65) | collective-permute-done | bytes 1441824 | tf_op jit(solution)/shard_map/ppermute | solution.py:72
  669.5 4.4 all-to-all-start.4
  678.1 27.5 %collective-permute-done.45 = bf16[128,2048]{1,0:T(8,128)(2,1)} collective-permute-done((bf16[128,2048]{1,0:T(8,128)(2,1)}, bf16[128,2048]{1,0:T(8,128)(2,1)}, u32[]{:S(2)}, u32[]{:S(2)}) %collective-permute-start.45) | collective-permute-done | bytes 524320 | tf_op jit(solution)/shard_map/ppermute | solution.py:72
  707.0 8.8 collective-permute-done.44
  722.2 5.9 collective-permute-done.46
  728.2 5.1 collective-permute-start.58
  735.0 4.6 fusion.154
  746.6 4.6 collective-permute-done.57
  760.0 8.0 reshape.692
  768.1 5.0 fusion.144
  774.3 4.2 squeeze.149
  795.3 6.0 fusion.36
  801.6 6.2 collective-permute-done.63
  807.8 30.6 %collective-permute-done.62 = bf16[128,2048]{1,0:T(8,128)(2,1)} collective-permute-done((bf16[128,2048]{1,0:T(8,128)(2,1)}, bf16[128,2048]{1,0:T(8,128)(2,1)}, u32[]{:S(2)}, u32[]{:S(2)}) %collective-permute-start.62) | collective-permute-done | bytes 524320 | tf_op jit(solution)/shard_map/ppermute | solution.py:72
  864.3 4.7 collective-permute-done.56
  869.0 6.8 collective-permute-done.55
  (519 shorter events, 281.2 us)
Async XLA Ops:
  7.2 144.1 %all-gather.19.cloned.1.call-start = ((), (), s32[]{:S(2)}) async-start(), calls=%async_computation.9 | async-start | bytes 2621440 | tf_op jit(solution)/shard_map/all_gather | solution.py:293
  8.0 147.4 %all-gather.11.cloned.1.call-start = ((), (), s32[]{:S(2)}) async-start(), calls=%async_computation.5 | async-start | bytes 6488064 | tf_op jit(solution)/shard_map/all_gather | solution.py:367
  11.9 69.9 %all-to-all-start = ((bf16[8,32,512]{2,1,0:T(8,128)(2,1)}), bf16[8,32,512]{2,1,0:T(8,128)(2,1)S(1)}, u32[]{:S(2)}, u32[]{:S(2)}) async-start(bf16[8,32,512]{2,1,0:T(8,128)(2,1)} %reshape.667), calls=%async_computation | async-start | bytes 524288 | tf_op jit(solution)/shard_map/all_to_all | solution.py:373
  81.8 66.5 %all-to-all-start.1 = ((bf16[2,8,64,704]{3,2,0,1:T(8,128)(2,1)}), bf16[2,8,64,704]{3,2,0,1:T(8,128)(2,1)}, u32[]{:S(2)}, u32[]{:S(2)}) async-start(bf16[2,8,64,704]{3,2,0,1:T(8,128)(2,1)} %copy.172), calls=%async_computation.1 | async-start | bytes 3145728 | tf_op jit(solution)/shard_map/all_to_all | solution.py:383
  86.1 129.1 %all-gather.17.cloned.1.call-start = ((), (), s32[]{:S(2)}) async-start(), calls=%async_computation.8 | async-start | bytes 1310720 | tf_op jit(solution)/shard_map/all_gather | solution.py:376
  86.9 241.8 %all-gather.21.cloned.1.call-start = ((), (), s32[]{:S(2)}) async-start(), calls=%async_computation.10 | async-start | bytes 7864320 | tf_op jit(solution)/shard_map/all_gather | solution.py:385
  151.0 231.9 %all-gather.13.cloned.1.call-start = ((), (), s32[]{:S(2)}) async-start(), calls=%async_computation.6 | async-start | bytes 3604480 | tf_op jit(solution)/shard_map/all_gather | solution.py:384
  153.8 26.4 %collective-permute-start.8 = (bf16[2,128,2048]{2,1,0:T(8,128)(2,1)}, bf16[2,128,2048]{2,1,0:T(8,128)(2,1)}, u32[]{:S(2)}, u32[]{:S(2)}) collective-permute-start(bf16[2,128,2048]{2,1,0:T(8,128)(2,1)} %dynamic-slice_bitcast_fusion), channel_id=1, source_target_pairs={{0,1},{1,0},{2,3},{3,2},{4,5},{5,4},{6,7},{7,6},{8,9},{9,8},{10,11... | collective-permute-start | bytes 3145736 | tf_op jit(solution)/shard_map/ppermute | solution.py:72
  169.7 39.1 %collective-permute-start.1 = (bf16[128,2048]{1,0:T(8,128)(2,1)S(1)}, bf16[128,2048]{1,0:T(8,128)(2,1)S(1)}, u32[]{:S(2)}, u32[]{:S(2)}) collective-permute-start(bf16[128,2048]{1,0:T(8,128)(2,1)S(1)} %get-tuple-element.114), channel_id=1, source_target_pairs={{0,1},{1,0},{4,5},{5,4},{2,3},{3,2},{6,7},{7,6},{8,9},{9,8},{12,13... | collective-permute-start | bytes 1572872 | tf_op jit(solution)/shard_map/ppermute | solution.py:72
  170.2 39.4 %collective-permute-start.2 = (bf16[128,2048]{1,0:T(8,128)(2,1)S(1)}, bf16[128,2048]{1,0:T(8,128)(2,1)S(1)}, u32[]{:S(2)}, u32[]{:S(2)}) collective-permute-start(bf16[128,2048]{1,0:T(8,128)(2,1)S(1)} %get-tuple-element.114), channel_id=1, source_target_pairs={{0,4},{1,5},{4,0},{5,1},{2,6},{3,7},{6,2},{7,3},{8,12},{9,13},{12,... | collective-permute-start | bytes 1572872 | tf_op jit(solution)/shard_map/ppermute | solution.py:72
  181.6 29.4 %collective-permute-start.3 = (bf16[128,2048]{1,0:T(8,128)(2,1)S(1)}, bf16[128,2048]{1,0:T(8,128)(2,1)S(1)}, u32[]{:S(2)}, u32[]{:S(2)}) collective-permute-start(bf16[128,2048]{1,0:T(8,128)(2,1)S(1)} %get-tuple-element.114), channel_id=1, source_target_pairs={{0,5},{1,4},{4,1},{5,0},{2,7},{3,6},{6,3},{7,2},{8,13},{9,12},{12,... | collective-permute-start | bytes 1572872 | tf_op jit(solution)/shard_map/ppermute | solution.py:72
  185.5 26.4 %collective-permute-start.4 = (bf16[128,2048]{1,0:T(8,128)(2,1)S(1)}, bf16[128,2048]{1,0:T(8,128)(2,1)S(1)}, u32[]{:S(2)}, u32[]{:S(2)}) collective-permute-start(bf16[128,2048]{1,0:T(8,128)(2,1)S(1)} %get-tuple-element.114), channel_id=1, source_target_pairs={{0,2},{2,0},{1,3},{3,1},{4,6},{6,4},{5,7},{7,5},{8,10},{10,8},{9,1... | collective-permute-start | bytes 1572872 | tf_op jit(solution)/shard_map/ppermute | solution.py:72
  232.4 44.3 %collective-permute-start.9 = (bf16[4,128,2048]{2,1,0:T(8,128)(2,1)}, bf16[4,128,2048]{2,1,0:T(8,128)(2,1)}, u32[]{:S(2)}, u32[]{:S(2)}) collective-permute-start(bf16[4,128,2048]{2,1,0:T(8,128)(2,1)} %bitcast.23), channel_id=1, source_target_pairs={{0,2},{2,0},{1,3},{3,1},{4,6},{6,4},{5,7},{7,5},{8,10},{10,8},{9,1... | collective-permute-start | bytes 6291464 | tf_op jit(solution)/shard_map/ppermute | solution.py:72
  232.9 38.3 %collective-permute-start.25 = (bf16[128,2048]{1,0:T(8,128)(2,1)S(1)}, bf16[128,2048]{1,0:T(8,128)(2,1)}, u32[]{:S(2)}, u32[]{:S(2)}) collective-permute-start(bf16[128,2048]{1,0:T(8,128)(2,1)S(1)} %copy-done.41), channel_id=1, source_target_pairs={{0,16},{8,24},{16,0},{24,8},{1,17},{9,25},{17,1},{25,9},{2,18},{10... | collective-permute-start | bytes 1572872 | tf_op jit(solution)/shard_map/ppermute | solution.py:72
  234.7 40.3 %collective-permute-start.26 = (bf16[128,2048]{1,0:T(8,128)(2,1)S(1)}, bf16[128,2048]{1,0:T(8,128)(2,1)S(1)}, u32[]{:S(2)}, u32[]{:S(2)}) collective-permute-start(bf16[128,2048]{1,0:T(8,128)(2,1)S(1)} %copy-done.41), channel_id=1, source_target_pairs={{0,24},{8,16},{16,8},{24,0},{1,25},{9,17},{17,9},{25,1},{2,26},{10... | collective-permute-start | bytes 1572872 | tf_op jit(solution)/shard_map/ppermute | solution.py:72
  237.3 46.6 %collective-permute-start.27 = (bf16[128,2048]{1,0:T(8,128)(2,1)S(1)}, bf16[128,2048]{1,0:T(8,128)(2,1)}, u32[]{:S(2)}, u32[]{:S(2)}) collective-permute-start(bf16[128,2048]{1,0:T(8,128)(2,1)S(1)} %copy-done.41), channel_id=1, source_target_pairs={{0,2},{2,0},{1,3},{3,1},{4,6},{6,4},{5,7},{7,5},{8,10},{10,8},{9,1... | collective-permute-start | bytes 1572872 | tf_op jit(solution)/shard_map/ppermute | solution.py:72
  256.7 29.1 %collective-permute-start.28 = (bf16[128,2048]{1,0:T(8,128)(2,1)}, bf16[128,2048]{1,0:T(8,128)(2,1)S(1)}, u32[]{:S(2)}, u32[]{:S(2)}) collective-permute-start(bf16[128,2048]{1,0:T(8,128)(2,1)} %collective-permute-done.24), channel_id=1, source_target_pairs={{0,2},{2,0},{1,3},{3,1},{4,6},{6,4},{5,7},{7,5},{8,10},{10,8},{9,1... | collective-permute-start | bytes 1572872 | tf_op jit(solution)/shard_map/ppermute | solution.py:72
  281.4 41.5 %collective-permute-start.11 = (bf16[128,2048]{1,0:T(8,128)(2,1)S(1)}, bf16[128,2048]{1,0:T(8,128)(2,1)S(1)}, u32[]{:S(2)}, u32[]{:S(2)}) collective-permute-start(bf16[128,2048]{1,0:T(8,128)(2,1)S(1)} %get-tuple-element.103), channel_id=1, source_target_pairs={{0,4},{1,5},{4,0},{5,1},{2,6},{3,7},{6,2},{7,3},{8,12},{9,13},{12,... | collective-permute-start | bytes 1572872 | tf_op jit(solution)/shard_map/ppermute | solution.py:72
  283.9 39.0 %collective-permute-start.10 = (bf16[128,2048]{1,0:T(8,128)(2,1)S(1)}, bf16[128,2048]{1,0:T(8,128)(2,1)S(1)}, u32[]{:S(2)}, u32[]{:S(2)}) collective-permute-start(bf16[128,2048]{1,0:T(8,128)(2,1)S(1)} %get-tuple-element.101), channel_id=1, source_target_pairs={{0,1},{1,0},{4,5},{5,4},{2,3},{3,2},{6,7},{7,6},{8,9},{9,8},{12,13... | collective-permute-start | bytes 1572872 | tf_op jit(solution)/shard_map/ppermute | solution.py:72
  285.8 42.1 %collective-permute-start.30 = (bf16[128,2048]{1,0:T(8,128)(2,1)S(1)}, bf16[128,2048]{1,0:T(8,128)(2,1)S(1)}, u32[]{:S(2)}, u32[]{:S(2)}) collective-permute-start(bf16[128,2048]{1,0:T(8,128)(2,1)S(1)} %copy-done.51), channel_id=1, source_target_pairs={{0,2},{2,0},{1,3},{3,1},{4,6},{6,4},{5,7},{7,5},{8,10},{10,8},{9,1... | collective-permute-start | bytes 1572872 | tf_op jit(solution)/shard_map/ppermute | solution.py:72
  331.9 38.3 %collective-permute-start.14 = (bf16[128,2048]{1,0:T(8,128)(2,1)S(1)}, bf16[128,2048]{1,0:T(8,128)(2,1)S(1)}, u32[]{:S(2)}, u32[]{:S(2)}) collective-permute-start(bf16[128,2048]{1,0:T(8,128)(2,1)S(1)} %get-tuple-element.42), channel_id=1, source_target_pairs={{0,16},{8,24},{16,0},{24,8},{1,17},{9,25},{17,1},{25,9},{2,18},{10... | collective-permute-start | bytes 1572872 | tf_op jit(solution)/shard_map/ppermute | solution.py:72
  332.9 37.4 %collective-permute-start.15 = (bf16[128,2048]{1,0:T(8,128)(2,1)S(1)}, bf16[128,2048]{1,0:T(8,128)(2,1)S(1)}, u32[]{:S(2)}, u32[]{:S(2)}) collective-permute-start(bf16[128,2048]{1,0:T(8,128)(2,1)S(1)} %get-tuple-element.42), channel_id=1, source_target_pairs={{0,24},{8,16},{16,8},{24,0},{1,25},{9,17},{17,9},{25,1},{2,26},{10... | collective-permute-start | bytes 1572872 | tf_op jit(solution)/shard_map/ppermute | solution.py:72
  334.9 36.0 %collective-permute-start.16 = (bf16[128,2048]{1,0:T(8,128)(2,1)S(1)}, bf16[128,2048]{1,0:T(8,128)(2,1)S(1)}, u32[]{:S(2)}, u32[]{:S(2)}) collective-permute-start(bf16[128,2048]{1,0:T(8,128)(2,1)S(1)} %get-tuple-element.42), channel_id=1, source_target_pairs={{0,2},{2,0},{1,3},{3,1},{4,6},{6,4},{5,7},{7,5},{8,10},{10,8},{9,1... | collective-permute-start | bytes 1572872 | tf_op jit(solution)/shard_map/ppermute | solution.py:72
  346.5 24.5 %collective-permute-start.17 = (bf16[128,2048]{1,0:T(8,128)(2,1)S(1)}, bf16[128,2048]{1,0:T(8,128)(2,1)S(1)}, u32[]{:S(2)}, u32[]{:S(2)}) collective-permute-start(bf16[128,2048]{1,0:T(8,128)(2,1)S(1)} %collective-permute-done.13), channel_id=1, source_target_pairs={{0,2},{2,0},{1,3},{3,1},{4,6},{6,4},{5,7},{7,5},{8,10},{10,8},{9,1... | collective-permute-start | bytes 1572872 | tf_op jit(solution)/shard_map/ppermute | solution.py:72
  412.4 69.8 %collective-permute-start.33 = (bf16[128,2048]{1,0:T(8,128)(2,1)}, bf16[128,2048]{1,0:T(8,128)(2,1)}, u32[]{:S(2)}, u32[]{:S(2)}) collective-permute-start(bf16[128,2048]{1,0:T(8,128)(2,1)} %get-tuple-element.97), channel_id=1, source_target_pairs={{0,16},{8,24},{16,0},{24,8},{1,17},{9,25},{17,1},{25,9},{2,18},{10... | collective-permute-start | bytes 1572872 | tf_op jit(solution)/shard_map/ppermute | solution.py:72
  420.9 61.3 %collective-permute-start.32 = (bf16[128,2048]{1,0:T(8,128)(2,1)}, bf16[128,2048]{1,0:T(8,128)(2,1)}, u32[]{:S(2)}, u32[]{:S(2)}) collective-permute-start(bf16[128,2048]{1,0:T(8,128)(2,1)} %get-tuple-element.95), channel_id=1, source_target_pairs={{0,8},{8,0},{16,24},{24,16},{1,9},{9,1},{17,25},{25,17},{2,10},{10... | collective-permute-start | bytes 1572872 | tf_op jit(solution)/shard_map/ppermute | solution.py:72
  425.1 57.0 %collective-permute-start.23 = (bf16[128,2048]{1,0:T(8,128)(2,1)}, bf16[128,2048]{1,0:T(8,128)(2,1)}, u32[]{:S(2)}, u32[]{:S(2)}) collective-permute-start(bf16[128,2048]{1,0:T(8,128)(2,1)} %get-tuple-element.99), channel_id=1, source_target_pairs={{0,24},{8,16},{16,8},{24,0},{1,25},{9,17},{17,9},{25,1},{2,26},{10... | collective-permute-start | bytes 1572872 | tf_op jit(solution)/shard_map/ppermute | solution.py:72
  427.5 77.1 %collective-permute-start.22 = (bf16[128,2048]{1,0:T(8,128)(2,1)}, bf16[128,2048]{1,0:T(8,128)(2,1)}, u32[]{:S(2)}, u32[]{:S(2)}) collective-permute-start(bf16[128,2048]{1,0:T(8,128)(2,1)} %get-tuple-element.100), channel_id=1, source_target_pairs={{0,16},{8,24},{16,0},{24,8},{1,17},{9,25},{17,1},{25,9},{2,18},{10... | collective-permute-start | bytes 1572872 | tf_op jit(solution)/shard_map/ppermute | solution.py:72
  429.4 75.1 %collective-permute-start.21 = (bf16[128,2048]{1,0:T(8,128)(2,1)}, bf16[128,2048]{1,0:T(8,128)(2,1)}, u32[]{:S(2)}, u32[]{:S(2)}) collective-permute-start(bf16[128,2048]{1,0:T(8,128)(2,1)} %get-tuple-element.98), channel_id=1, source_target_pairs={{0,8},{8,0},{16,24},{24,16},{1,9},{9,1},{17,25},{25,17},{2,10},{10... | collective-permute-start | bytes 1572872 | tf_op jit(solution)/shard_map/ppermute | solution.py:72
  512.4 24.2 %collective-permute-start.37 = (bf16[128,2048]{1,0:T(8,128)(2,1)S(1)}, bf16[128,2048]{1,0:T(8,128)(2,1)S(1)}, u32[]{:S(2)}, u32[]{:S(2)}) collective-permute-start(bf16[128,2048]{1,0:T(8,128)(2,1)S(1)} %get-tuple-element.34), channel_id=1, source_target_pairs={{0,5},{1,4},{4,1},{5,0},{2,7},{3,6},{6,3},{7,2},{8,13},{9,12},{12,... | collective-permute-start | bytes 1572872 | tf_op jit(solution)/shard_map/ppermute | solution.py:72
  577.0 34.1 %collective-permute-start.42 = (bf16[4,128,2048]{2,1,0:T(8,128)(2,1)}, bf16[4,128,2048]{2,1,0:T(8,128)(2,1)}, u32[]{:S(2)}, u32[]{:S(2)}) collective-permute-start(bf16[4,128,2048]{2,1,0:T(8,128)(2,1)} %bitcast.353), channel_id=1, source_target_pairs={{0,2},{2,0},{1,3},{3,1},{4,6},{6,4},{5,7},{7,5},{8,10},{10,8},{9,1... | collective-permute-start | bytes 6291464 | tf_op jit(solution)/shard_map/ppermute | solution.py:72
  591.1 38.5 %collective-permute-start.66 = (bf16[2,8,64,704]{3,2,1,0:T(8,128)(2,1)}, bf16[2,8,64,704]{3,2,1,0:T(8,128)(2,1)}, u32[]{:S(2)}, u32[]{:S(2)}) collective-permute-start(bf16[2,8,64,704]{3,2,1,0:T(8,128)(2,1)} %get-tuple-element.59), channel_id=1, source_target_pairs={{0,5},{1,4},{4,1},{5,0},{2,7},{3,6},{6,3},{7,2},{8,13},{9,12},{12,... | collective-permute-start | bytes 4325384 | tf_op jit(solution)/shard_map/ppermute | solution.py:72
  592.6 70.8 %collective-permute-start.65 = (bf16[2,8,64,704]{3,2,1,0:T(8,128)(2,1)}, bf16[2,8,64,704]{3,2,1,0:T(8,128)(2,1)}, u32[]{:S(2)}, u32[]{:S(2)}) collective-permute-start(bf16[2,8,64,704]{3,2,1,0:T(8,128)(2,1)} %get-tuple-element.58), channel_id=1, source_target_pairs={{0,4},{1,5},{4,0},{5,1},{2,6},{3,7},{6,2},{7,3},{8,12},{9,13},{12,... | collective-permute-start | bytes 4325384 | tf_op jit(solution)/shard_map/ppermute | solution.py:72
  594.1 69.8 %collective-permute-start.64 = (bf16[2,8,64,704]{3,2,1,0:T(8,128)(2,1)}, bf16[2,8,64,704]{3,2,1,0:T(8,128)(2,1)}, u32[]{:S(2)}, u32[]{:S(2)}) collective-permute-start(bf16[2,8,64,704]{3,2,1,0:T(8,128)(2,1)} %get-tuple-element.57), channel_id=1, source_target_pairs={{0,1},{1,0},{4,5},{5,4},{2,3},{3,2},{6,7},{7,6},{8,9},{9,8},{12,13... | collective-permute-start | bytes 4325384 | tf_op jit(solution)/shard_map/ppermute | solution.py:72
  601.6 139.2 %collective-permute-start.69 = (bf16[176,2048]{1,0:T(8,128)(2,1)}, bf16[176,2048]{1,0:T(8,128)(2,1)}, u32[]{:S(2)}, u32[]{:S(2)}) collective-permute-start(bf16[176,2048]{1,0:T(8,128)(2,1)} %get-tuple-element.63), channel_id=1, source_target_pairs={{0,5},{1,4},{4,1},{5,0},{2,7},{3,6},{6,3},{7,2},{8,13},{9,12},{12,... | collective-permute-start | bytes 2162696 | tf_op jit(solution)/shard_map/ppermute | solution.py:72
  611.1 130.7 %collective-permute-start.68 = (bf16[176,2048]{1,0:T(8,128)(2,1)}, bf16[176,2048]{1,0:T(8,128)(2,1)}, u32[]{:S(2)}, u32[]{:S(2)}) collective-permute-start(bf16[176,2048]{1,0:T(8,128)(2,1)} %get-tuple-element.64), channel_id=1, source_target_pairs={{0,4},{1,5},{4,0},{5,1},{2,6},{3,7},{6,2},{7,3},{8,12},{9,13},{12,... | collective-permute-start | bytes 2162696 | tf_op jit(solution)/shard_map/ppermute | solution.py:72
  629.6 75.9 %collective-permute-start.45 = (bf16[128,2048]{1,0:T(8,128)(2,1)}, bf16[128,2048]{1,0:T(8,128)(2,1)}, u32[]{:S(2)}, u32[]{:S(2)}) collective-permute-start(bf16[128,2048]{1,0:T(8,128)(2,1)} %get-tuple-element.89), channel_id=1, source_target_pairs={{0,5},{1,4},{4,1},{5,0},{2,7},{3,6},{6,3},{7,2},{8,13},{9,12},{12,... | collective-permute-start | bytes 1572872 | tf_op jit(solution)/shard_map/ppermute | solution.py:72
  663.4 52.5 %collective-permute-start.44 = (bf16[128,2048]{1,0:T(8,128)(2,1)}, bf16[128,2048]{1,0:T(8,128)(2,1)}, u32[]{:S(2)}, u32[]{:S(2)}) collective-permute-start(bf16[128,2048]{1,0:T(8,128)(2,1)} %get-tuple-element.90), channel_id=1, source_target_pairs={{0,4},{1,5},{4,0},{5,1},{2,6},{3,7},{6,2},{7,3},{8,12},{9,13},{12,... | collective-permute-start | bytes 1572872 | tf_op jit(solution)/shard_map/ppermute | solution.py:72
  663.9 54.5 %collective-permute-start.43 = (bf16[128,2048]{1,0:T(8,128)(2,1)}, bf16[128,2048]{1,0:T(8,128)(2,1)}, u32[]{:S(2)}, u32[]{:S(2)}) collective-permute-start(bf16[128,2048]{1,0:T(8,128)(2,1)} %get-tuple-element.88), channel_id=1, source_target_pairs={{0,1},{1,0},{4,5},{5,4},{2,3},{3,2},{6,7},{7,6},{8,9},{9,8},{12,13... | collective-permute-start | bytes 1572872 | tf_op jit(solution)/shard_map/ppermute | solution.py:72
  669.5 83.7 %all-to-all-start.4 = ((bf16[2,8,64,704]{3,2,0,1:T(8,128)(2,1)}), bf16[2,8,64,704]{3,2,0,1:T(8,128)(2,1)S(1)}, u32[]{:S(2)}, u32[]{:S(2)}) async-start(bf16[2,8,64,704]{3,2,0,1:T(8,128)(2,1)} %copy.196), calls=%async_computation.4 | async-start | bytes 3145728 | tf_op jit(solution)/shard_map/all_to_all | solution.py:491
  673.9 182.4 %all-gather.15.cloned.1.call-start = ((), (), s32[]{:S(2)}) async-start(), calls=%async_computation.7 | async-start | bytes 3538944 | tf_op jit(solution)/shard_map/all_gather | solution.py:547
  705.5 36.8 %collective-permute-start.67 = (bf16[176,2048]{1,0:T(8,128)(2,1)S(1)}, bf16[176,2048]{1,0:T(8,128)(2,1)}, u32[]{:S(2)}, u32[]{:S(2)}) collective-permute-start(bf16[176,2048]{1,0:T(8,128)(2,1)S(1)} %get-tuple-element.62), channel_id=1, source_target_pairs={{0,1},{1,0},{4,5},{5,4},{2,3},{3,2},{6,7},{7,6},{8,9},{9,8},{12,13... | collective-permute-start | bytes 2162696 | tf_op jit(solution)/shard_map/ppermute | solution.py:72
  715.9 30.7 %collective-permute-start.59 = (bf16[8,32,512]{2,1,0:T(8,128)(2,1)}, bf16[8,32,512]{2,1,0:T(8,128)(2,1)}, u32[]{:S(2)}, u32[]{:S(2)}) collective-permute-start(bf16[8,32,512]{2,1,0:T(8,128)(2,1)} %get-tuple-element.86), channel_id=1, source_target_pairs={{0,24},{8,16},{16,8},{24,0},{1,25},{9,17},{17,9},{25,1},{2,26},{10... | collective-permute-start | bytes 786440 | tf_op jit(solution)/shard_map/ppermute | solution.py:72
  741.8 45.7 %collective-permute-start.60 = (bf16[2,128,2048]{2,1,0:T(8,128)(2,1)}, bf16[2,128,2048]{2,1,0:T(8,128)(2,1)}, u32[]{:S(2)}, u32[]{:S(2)}) collective-permute-start(bf16[2,128,2048]{2,1,0:T(8,128)(2,1)} %fusion.27), channel_id=1, source_target_pairs={{0,1},{1,0},{2,3},{3,2},{4,5},{5,4},{6,7},{7,6},{8,9},{9,8},{10,11... | collective-permute-start | bytes 3145736 | tf_op jit(solution)/shard_map/ppermute | solution.py:72
  754.4 31.1 %all-to-all-start.3 = ((bf16[8,32,512]{2,1,0:T(8,128)(2,1)}), bf16[8,32,512]{2,1,0:T(8,128)(2,1)S(1)}, u32[]{:S(2)}, u32[]{:S(2)}) async-start(bf16[8,32,512]{2,1,0:T(8,128)(2,1)} %fusion.93), calls=%async_computation.3 | async-start | bytes 524288 | tf_op jit(solution)/shard_map/all_to_all | solution.py:537
  793.8 44.5 %collective-permute-start.62 = (bf16[128,2048]{1,0:T(8,128)(2,1)}, bf16[128,2048]{1,0:T(8,128)(2,1)}, u32[]{:S(2)}, u32[]{:S(2)}) collective-permute-start(bf16[128,2048]{1,0:T(8,128)(2,1)} %get-tuple-element.83), channel_id=1, source_target_pairs={{0,16},{8,24},{16,0},{24,8},{1,17},{9,25},{17,1},{25,9},{2,18},{10... | collective-permute-start | bytes 1572872 | tf_op jit(solution)/shard_map/ppermute | solution.py:72
  793.8 44.5 %collective-permute-start.61 = (bf16[128,2048]{1,0:T(8,128)(2,1)}, bf16[128,2048]{1,0:T(8,128)(2,1)}, u32[]{:S(2)}, u32[]{:S(2)}) collective-permute-start(bf16[128,2048]{1,0:T(8,128)(2,1)} %get-tuple-element.82), channel_id=1, source_target_pairs={{0,8},{8,0},{16,24},{24,16},{1,9},{9,1},{17,25},{25,17},{2,10},{10... | collective-permute-start | bytes 1572872 | tf_op jit(solution)/shard_map/ppermute | solution.py:72
  801.5 39.9 %collective-permute-start.47 = (f32[4,2,2,160]{3,2,1,0:T(2,128)S(1)}, f32[4,2,2,160]{3,2,1,0:T(2,128)S(1)}, u32[]{:S(2)}, u32[]{:S(2)}) collective-permute-start(f32[4,2,2,160]{3,2,1,0:T(2,128)S(1)} %dynamic-slice_bitcast_fusion.1), channel_id=1, source_target_pairs={{0,2},{2,0},{1,3},{3,1},{4,6},{6,4},{5,7},{7,5},{8,10},{10,8},{9,1... | collective-permute-start | bytes 30728 | tf_op jit(solution)/shard_map/ppermute | solution.py:72
  (118 other events, 2352.3 us)
Sparse Core Ops, SparseCore 0:
  9.6 49.6 all-gather.18
  62.8 88.2 all-gather.10
  153.3 25.9 all-gather.16
  181.0 78.1 all-gather.20
  260.9 61.1 all-gather.12
  735.1 45.5 all-gather.14
